TPU v7x, 512 devices: a whole 4x4x16 slice. The times are simulated.
512 devices in a mesh: group: 16 (over z), replica: 32 (over y, x, core).
Axes of the slice: x: 4, y: 4, z: 16, core: 2. Of those that a mesh axis runs over, the one named last changes fastest.
Arguments:
- gradient: bfloat16 [512, 32, 20480], P(('group', 'replica')), may hold values from -24 to 24
- residual: bfloat16 [512, 32, 20480], P(('group', 'replica')), may hold values from -4 to 4
- q_prev: float32 [20480, 16], P(('group', 'replica')), may hold values from -6 to 6
- p_bits: int32 [512, 32, 16], P(('group', 'replica')), may hold values from 0 to 2097151
- q_bits: int32 [512, 20480, 8], P(('group', 'replica')), may hold values from 0 to 8191
Outputs:
- q_next: float32 [20480, 16], P(('group', 'replica'))
- new_residual: bfloat16 [512, 32, 20480], P(('group', 'replica'))
All inputs are finite; a program needn't handle non-finite values.
Results may differ from a plain program's by a relative error of at most 0.012.
Values sent between devices are 32-bit elements; how exact they have to be, the bound alone decides.
No kernel may reach another device: no remote copies, remote signals or barrier semaphores. Data moves between devices by JAX's collectives and lax.ppermute only.
A program may use at most 64 MiB of HBM per device.

v0:
```python
import jax
import jax.numpy as jnp
from jax import lax
from jax.sharding import PartitionSpec as P

dither_width = 2.0 ** (-2)


def orthonormal(matrix):
    columns = []
    for index in range(matrix.shape[1]):
        vector = matrix[:, index]
        for earlier in columns:
            vector = vector - jnp.sum(earlier * vector) * earlier
        columns.append(vector * lax.rsqrt(jnp.sum(vector * vector)))
    return jnp.stack(columns, axis=1)


def dithered(local, noise):
    return (local + noise * dither_width * jnp.abs(local)).astype(jnp.bfloat16)


def outer_product(basis, factor):
    return lax.dot_general(
        basis,
        factor,
        (((1,), (1,)), ((), ())),
        precision=lax.Precision.HIGHEST,
        preferred_element_type=jnp.float32,
    )


def shards(gradient, residual, q_prev, p_bits, q_bits):
    merged = gradient[0].astype(jnp.float32) + residual[0].astype(jnp.float32)
    local_p = jnp.dot(
        merged,
        lax.all_gather(q_prev, ("group", "replica"), axis=0, tiled=True),
        precision=lax.Precision.HIGHEST,
        preferred_element_type=jnp.float32,
    )
    noise_p = p_bits[0].astype(jnp.float32) * 2.0 ** (-21) - 0.5
    wide_p = dithered(local_p, noise_p).astype(jnp.float32)
    total_p = lax.psum(wide_p, ("group", "replica"))
    basis = orthonormal(total_p)
    local_q = lax.dot_general(
        merged,
        basis,
        (((0,), (0,)), ((), ())),
        precision=lax.Precision.HIGHEST,
        preferred_element_type=jnp.float32,
    )
    words = q_bits[0]
    low = (words % 128).astype(jnp.float32) / 128.0
    high = (words // 128).astype(jnp.float32) / 64.0
    noise_q = jnp.concatenate([low, high], axis=1) - 0.5
    wide_q = dithered(local_q, noise_q).astype(jnp.float32)
    world = lax.axis_size(("group", "replica"))
    place = lax.axis_index(("group", "replica"))
    share = wide_q.shape[0] // world
    total_q = lax.psum(wide_q, ("group", "replica"))
    mine = lax.dynamic_slice_in_dim(total_q, place * share, share, 0)
    mean_q = total_q / world
    updated = merged - outer_product(basis, mean_q)
    q_next = mine * world ** (-0.5)
    return (q_next, updated.astype(jnp.bfloat16)[None])


def solution(mesh):
    in_specs = (
        P(("group", "replica"), None, None),
        P(("group", "replica"), None, None),
        P(("group", "replica"), None),
        P(("group", "replica"), None, None),
        P(("group", "replica"), None, None),
    )
    out_specs = (P(("group", "replica"), None), P(("group", "replica"), None, None))
    return jax.shard_map(shards, mesh=mesh, in_specs=in_specs, out_specs=out_specs, check_vma=False)
```

profile of v0, /device:TPU:1, one launch (start us, length us, event | category | flops | bytes accessed | tf_op | source)
XLA Modules:
  0.0 1028.1 jit_solution(9168233245552362220)
XLA Ops:
  7.9 2.6 fusion.17
  10.6 205.6 %all-gather.3.cloned.1.call-done = f32[512,40,16]{1,2,0:T(8,128)} async-done(((f32[1,40,16]{1,2,0:T(8,128)}), f32[512,40,16]{1,2,0:T(8,128)}) %all-gather.3.cloned.1.call-update) | async-done | bytes 1310736 | tf_op jit(solution)/shard_map/all_gather | solution.py:37
  216.1 5.5 copy.8
  221.6 5.2 reshape.18
  226.9 3.6 fusion.28
  230.5 102.3 %psum.14 = f32[32,16]{0,1:T(8,128)S(1)} all-reduce(f32[32,16]{0,1:T(8,128)S(1)} %fusion.28), channel_id=1, replica_groups=mesh['group'=16,'replica'=32] {'group','replica'}, use_global_device_ids=true, to_apply=%region_0.0 | all-reduce | flops 512 | bytes 4096 | tf_op jit(solution)/shard_map/psum | solution.py:43
  338.7 8.8 multiply_reduce_fusion.14
  348.2 6.9 multiply_reduce_fusion.13
  355.1 3.8 multiply_reduce_fusion.97
  363.3 13.8 %multiply_reduce_fusion.12 = (f32[]{:T(128)}, f32[]{:T(128)}, f32[]{:T(128)}, f32[]{:T(128)}, f32[]{:T(128)}, /*index=5*/f32[]{:T(128)}, f32[]{:T(128)}, f32[]{:...) fusion(f32[32]{0:T(128)S(1)} %get-tuple-element.204, ...), kind=kLoop, calls=%fused_computation.119 | loop fusion | flops 2037 | bytes 3200 | tf_op jit(solution)/shard_map/reduce_sum | solution.py:14
  377.8 7.5 multiply_reduce_fusion.11
  392.2 11.3 %multiply_reduce_fusion.10 = (f32[]{:T(128)}, f32[]{:T(128)}, f32[]{:T(128)}, f32[]{:T(128)}, f32[]{:T(128)}, /*index=5*/f32[]{:T(128)}, f32[]{:T(128)}, f32[]{:...) fusion(f32[32]{0:T(128)S(1)} %get-tuple-element.187, ...), kind=kLoop, calls=%fused_computation.115 | loop fusion | flops 1655 | bytes 2664 | tf_op jit(solution)/shard_map/reduce_sum | solution.py:14
  404.1 7.7 multiply_reduce_fusion.9
  417.7 10.0 multiply_reduce_fusion.8
  428.4 5.7 multiply_reduce_fusion.7
  438.5 7.4 multiply_reduce_fusion.6
  446.7 4.4 multiply_reduce_fusion.5
  455.6 5.1 multiply_reduce_fusion.4
  461.2 3.2 multiply_reduce_fusion.3
  467.0 3.2 multiply_reduce_fusion.2
  475.7 75.0 %subtract_multiply_fusion = (f32[32,1]{0,1:T(1,128)S(1)}, f32[32,1]{0,1:T(1,128)S(1)}, f32[32,1]{0,1:T(1,128)S(1)}, f32[32,1]{0,1:T(1,128)S(1)}, f32[32,1]{0,1:T...) fusion(f32[32,1]{0,1:T(1,128)S(1)} %get-tuple-element.225, ...), kind=kLoop, calls=%fused_computation.96 | loop fusion | flops 8160 | bytes 4508 | tf_op jit(solution)/shard_map/mul | solution.py:15
  550.8 4.0 fusion.13
  554.8 460.3 %all-reduce.2.cloned.1.call-done = f32[20480,16]{0,1:T(8,128)} async-done(((f32[20480,16]{0,1:T(8,128)}), f32[20480,16]{0,1:T(8,128)}) %all-reduce.2.cloned.1.call-update) | async-done | bytes 1310736 | tf_op jit(solution)/shard_map/psum | solution.py:60
  1015.1 4.8 fusion.1
  (32 shorter events, 35.4 us)
Async XLA Ops:
  7.2 209.0 %all-gather.3.cloned.1.call-start = ((), (), s32[]{:S(2)}) async-start(), calls=%async_computation.1 | async-start | bytes 4202496 | tf_op jit(solution)/shard_map/all_gather | solution.py:37
  7.9 1007.2 %all-reduce.2.cloned.1.call-start = ((), (), s32[]{:S(2)}) async-start(), calls=%async_computation | async-start | bytes 2621440 | tf_op jit(solution)/shard_map/psum | solution.py:60
  221.6 5.2 copy-start
  221.6 5.2 copy-start.1
  221.6 5.2 copy-start.2
Sparse Core Ops, SparseCore 0:
  12.6 203.4 all-gather.2
  554.9 460.1 all-reduce.1
where the time goes:
time: 1030 us
  waiting for transfers between devices  667 us (65%)
  other arithmetic  211 us (20%)
  blocking collectives  102 us (10%)
  between operations  24.9 us (2%)
  matrix products  12.4 us (1%)
  local copies, waits for them, and re-layouts  10.8 us (1%)
    psum x1, waiting for transfers between devices, shards(): total_q = lax.psum(wide_q, ('group', 'replica'))  460 us
    all_gather x1, waiting for transfers between devices, shards(): lax.all_gather(q_prev, ('group', 'replica'), axis=0, tiled=True)  206 us
    reduce_sum x25, other arithmetic, orthonormal(): vector = vector - jnp.sum(earlier * vector) * earlier  117 us
    psum x1, blocking collectives, shards(): total_p = lax.psum(wide_p, ('group', 'replica'))  102 us
    mul x1, other arithmetic, orthonormal(): columns.append(vector * lax.rsqrt(jnp.sum(vector * vector)))  75 us
  transfers between devices with their start and end apart: 2, of which 2 were waited for; matrix products, arithmetic and copies ran while one was open for 0% of the time, Pallas kernels for 0%

commit v1 on v0

v1 whole, which is shorter than its diff:
```python
import functools

import jax
import jax.numpy as jnp
from jax import lax
from jax.experimental import pallas as pl
from jax.experimental.pallas import tpu as pltpu
from jax.sharding import Mesh, PartitionSpec as P

FF = 20480
RANK = 16
ROWS = 32
WORLD = 512
HALF = FF // 2
BLOCK = 640
STEP = 2560
WIDTH = 0.25
F32 = jnp.float32
BF16 = jnp.bfloat16
VMEM_LIMIT = 48 * 1024 * 1024


def call(body, out_shape, **kw):
    return pl.pallas_call(
        body,
        out_shape=out_shape,
        compiler_params=pltpu.CompilerParams(vmem_limit_bytes=VMEM_LIMIT),
        **kw,
    )


def parts(x, n):
    out = []
    for _ in range(n):
        p = x.astype(BF16)
        out.append(p)
        x = x - p.astype(F32)
    return out


def spread_factor(x_ref, o_ref):
    halves = []
    for g in range(2):
        t = x_ref[g * 8 : g * 8 + 8].reshape(64, 128).T
        halves.append(jnp.concatenate([t[0:40], t[40:80]], axis=1))
    packed = jnp.concatenate(halves, axis=0)
    for s in range(o_ref.shape[0]):
        o_ref[s] = packed


def left_factor(c_ref, grad_ref, res_ref, own_ref, other_ref, bits_ref, o_ref):
    c = c_ref[0]
    lane = lax.broadcasted_iota(jnp.int32, (ROWS, 128), 1)
    owner = (lane % 64) // 8
    total = jnp.zeros((ROWS, 128), F32)
    for g in range(2):
        chunks = []
        for s in range(16):
            a = own_ref[s, g * 40 : g * 40 + 40, :]
            b = other_ref[s, g * 40 : g * 40 + 40, :]
            chunks.append(jnp.where(c == 0, a, b))
            chunks.append(jnp.where(c == 0, b, a))
        factor = jnp.concatenate(chunks, axis=0)
        factor = jnp.concatenate(parts(factor, 2), axis=1)
        rows = []
        for ref in (grad_ref, res_ref):
            for e in range(8):
                z = g * 8 + e
                rows.append(ref[:, z * 1280 : z * 1280 + 1280])
        wide = jnp.concatenate(rows, axis=0)
        prod = jnp.dot(wide, factor, preferred_element_type=F32)
        prod = prod[0:256] + prod[256:512]
        prod = prod[:, 0:128] + prod[:, 128:256]
        for e in range(8):
            total = total + jnp.where(owner == e, prod[e * 32 : e * 32 + 32], 0.0)
    rank = lax.broadcasted_iota(jnp.int32, (RANK, 128), 0)
    lane = lax.broadcasted_iota(jnp.int32, (RANK, 128), 1)
    fold = jnp.where((lane // 64) * 8 + lane % 8 == rank, 1.0, 0.0).astype(F32)
    local = lax.dot_general(
        fold, total, (((1,), (1,)), ((), ())), precision=lax.Precision.HIGHEST, preferred_element_type=F32
    )
    noise = bits_ref[...].astype(F32) * 2.0 ** (-21) - 0.5
    sent = (local + noise * WIDTH * jnp.abs(local)).astype(BF16).astype(F32)
    tile = jnp.concatenate([sent[0:8], sent[8:16], jnp.zeros((8, 64), F32)], axis=1)
    for s in range(o_ref.shape[0]):
        o_ref[s] = tile


def add_and_repeat(x_ref, o_ref):
    total = x_ref[0]
    for s in range(1, x_ref.shape[0]):
        total = total + x_ref[s]
    for s in range(o_ref.shape[0]):
        o_ref[s] = total


def orthonormal(rows):
    index = lax.broadcasted_iota(jnp.int32, (RANK, 1), 0)
    for j in range(RANK):
        vector = rows[j : j + 1]
        inner = jnp.sum(rows * vector, axis=1, keepdims=True)
        square = inner[j : j + 1]
        unit = vector * lax.rsqrt(square)
        later = jnp.where(index > j, inner / square, 0.0)
        rows = jnp.where(index == j, unit, rows - later * vector)
    return rows


def right_columns(basis, grad, res, words):
    split = jnp.concatenate(parts(basis, 3), axis=0)
    split = jnp.concatenate([split, split], axis=1)
    both = jnp.concatenate([grad, res], axis=0)
    prod = jnp.dot(split, both, preferred_element_type=F32)
    local = prod[0:16] + prod[16:32] + prod[32:48]
    low = (words & 127).astype(F32) * (1.0 / 128.0)
    high = (words >> 7).astype(F32) * (1.0 / 64.0)
    noise = jnp.concatenate([low, high], axis=0) - 0.5
    return (local + noise * WIDTH * jnp.abs(local)).astype(BF16).astype(F32)


def store_blocks(sent, o_ref):
    for t in range(STEP // BLOCK):
        o_ref[t] = sent[:, t * BLOCK : t * BLOCK + BLOCK]


def right_first(c_ref, tiles_ref, grad_ref, res_ref, words_ref, basis_ref, o_ref):
    @pl.when(pl.program_id(0) == 0)
    def _():
        total = tiles_ref[0]
        for s in range(1, tiles_ref.shape[0]):
            total = total + tiles_ref[s]
        rows = jnp.concatenate([total[:, 0:32], total[:, 32:64]], axis=0)
        basis_ref[...] = orthonormal(rows)

    sent = right_columns(basis_ref[...], grad_ref[...], res_ref[...], words_ref[...])
    store_blocks(sent, o_ref)


def right_second(c_ref, basis_ref, grad_ref, res_ref, words_ref, o_ref):
    sent = right_columns(basis_ref[...], grad_ref[...], res_ref[...], words_ref[...])
    store_blocks(sent, o_ref)


def update(where_ref, basis_ref, grad_ref, res_ref, own_ref, other_ref, q_ref, o_ref):
    c, block, offset = where_ref[0], where_ref[1], where_ref[2]
    high, low = parts(basis_ref[...].T, 2)
    left = jnp.concatenate([high, low, high], axis=1)

    def columns(total_ref, base):
        for t in range(HALF // BLOCK):
            mean = total_ref[t] * (1.0 / WORLD)
            mh, ml = parts(mean, 2)
            right = jnp.concatenate([mh, mh, ml], axis=0)
            approx = jnp.dot(left, right, preferred_element_type=F32)
            at = pl.ds(pl.multiple_of(base + t * BLOCK, 128), BLOCK)
            merged = grad_ref[:, at].astype(F32) + res_ref[:, at].astype(F32)
            o_ref[:, at] = (merged - approx).astype(BF16)

    columns(own_ref, c * HALF)
    columns(other_ref, (1 - c) * HALF)
    t = block % 16
    mine = jnp.where(block // 16 == c, own_ref[t], other_ref[t])
    mine = pltpu.roll(mine, (BLOCK - offset) % BLOCK, 1)
    q_ref[...] = mine[:, 0:40] * WORLD ** (-0.5)


def exchange(blocks, axis):
    return lax.all_to_all(blocks, axis, 0, 0, tiled=True)


def shards(gradient, residual, q_prev, p_bits, q_bits):
    z, plane, group = ("zh", "zl"), ("s", "c"), ("zl", "s")
    grad, res = gradient[0], residual[0]
    p_words, q_words = p_bits[0].T, q_bits[0].T
    c = lax.axis_index("c")
    device = lax.axis_index(("zh", "zl", "s", "c"))
    swap = [(0, 1), (1, 0)]
    whole = pl.BlockSpec(memory_space=pltpu.VMEM)
    scalars = pl.BlockSpec(memory_space=pltpu.SMEM)

    with jax.named_scope("gather_q_prev"):
        qt = q_prev.T
        piece = jnp.concatenate([qt[0:8], qt[8:16], jnp.zeros((8, 48), F32)], axis=1)
        pieces = exchange(jnp.broadcast_to(piece, (16, 8, 128)), z)
        spread = call(spread_factor, jax.ShapeDtypeStruct((16, 80, 128), F32), in_specs=[whole], out_specs=whole)(pieces)
        own = exchange(spread, "s")
        other = lax.ppermute(own, "c", swap)
    with jax.named_scope("left_factor"):
        tile = call(
            left_factor,
            jax.ShapeDtypeStruct((32, 8, 128), F32),
            in_specs=[scalars] + [whole] * 5,
            out_specs=whole,
        )(c.reshape(1), grad, res, own, other, p_words)
        tile = exchange(tile, plane)
        tile = call(add_and_repeat, jax.ShapeDtypeStruct((16, 8, 128), F32), in_specs=[whole], out_specs=whole)(tile)
        tile = exchange(tile, z)
    steps = HALF // STEP
    with jax.named_scope("right_factor"):

        def grid(fixed, side, out_specs):
            def place(i, c_ref):
                return (0, (c_ref[0] if side else 1 - c_ref[0]) * steps + i)

            return pltpu.PrefetchScalarGridSpec(
                num_scalar_prefetch=1,
                grid=(steps,),
                in_specs=[pl.BlockSpec(fixed, lambda i, c_ref: (0,) * len(fixed))]
                + [pl.BlockSpec((32, STEP), place), pl.BlockSpec((32, STEP), place), pl.BlockSpec((8, STEP), place)],
                out_specs=out_specs,
            )

        blocks = pl.BlockSpec((STEP // BLOCK, 16, BLOCK), lambda i, c_ref: (i, 0, 0))
        half = jax.ShapeDtypeStruct((16, 16, BLOCK), F32)
        basis, away = call(
            right_first,
            (jax.ShapeDtypeStruct((16, 32), F32), half),
            grid_spec=grid((16, 8, 128), False, (pl.BlockSpec((16, 32), lambda i, c_ref: (0, 0)), blocks)),
        )(c.reshape(1), tile, grad, res, q_words)
        away = lax.ppermute(away, "c", swap)
        kept = call(right_second, half, grid_spec=grid((16, 32), True, blocks))(c.reshape(1), basis, grad, res, q_words)
        summed = (kept + away).reshape(32, 8, BLOCK)
        summed = exchange(summed, group)
        summed = call(add_and_repeat, jax.ShapeDtypeStruct((8, 8, BLOCK), F32), in_specs=[whole], out_specs=whole)(summed)
        summed = exchange(summed, "zh")
        summed = call(add_and_repeat, jax.ShapeDtypeStruct((32, 8, BLOCK), F32), in_specs=[whole], out_specs=whole)(summed)
        total = exchange(summed, group).reshape(16, 16, BLOCK)
        rest = lax.ppermute(total, "c", swap)
    with jax.named_scope("update"):
        where = jnp.stack([c, device // 16, (device % 16) * 40])
        q_next, updated = call(
            update,
            (jax.ShapeDtypeStruct((16, 40), F32), jax.ShapeDtypeStruct((ROWS, FF), BF16)),
            in_specs=[scalars] + [whole] * 5,
            out_specs=(whole, whole),
        )(where, basis, grad, res, total, rest)
    return (q_next.T, updated[None])


def solution(mesh):
    every = ("zh", "zl", "s", "c")
    split = Mesh(mesh.devices.reshape(8, 2, 16, 2), every)
    row, block = P(every, None), P(every, None, None)
    return jax.shard_map(
        shards,
        mesh=split,
        in_specs=(block, block, row, block, block),
        out_specs=(row, block),
        check_vma=False,
    )
```

time: 1030 us -> 150 us (0.15)
  waiting for transfers between devices: 667 us -> 3.81 us
  other arithmetic: 211 us -> 0.22 us
  between operations: 24.9 us -> 0.76 us
  starting transfers between devices: 0.08 us -> 16.1 us
  blocking collectives: 102 us -> 116 us
  matrix products: 12.4 us -> 0 us
    psum x1 -> x0, waiting for transfers between devices: 460 us -> none  [shards(): total_q = lax.psum(wide_q, ('group', 'replica'))]
    all_gather x1 -> x0, waiting for transfers between devices: 206 us -> none  [shards(): lax.all_gather(q_prev, ('group', 'replica'), axis=0, tiled=True)]
    reduce_sum x34 -> x0, other arithmetic: 132 us -> none  [the longest x25 117 us: orthonormal(): vector = vector - jnp.sum(earlier * vector) * earlier]
    all_to_all x0 -> x7, blocking collectives: none -> 116 us  [exchange(): return lax.all_to_all(blocks, axis, 0, 0, tiled=True)]
    psum x1 -> x0, blocking collectives: 102 us -> none  [shards(): total_p = lax.psum(wide_p, ('group', 'replica'))]
    mul x2 -> x0, other arithmetic: 76.4 us -> none  [the longest x1 75 us: orthonormal(): columns.append(vector * lax.rsqrt(jnp.sum(vector * vector)))]
    ppermute x0 -> x3, starting transfers between devices: none -> 16.1 us  [the longest x1 6.98 us: shards(): rest = lax.ppermute(total, 'c', swap)]
    dot_general x3 -> x0, matrix products: 12.4 us -> none  [the longest x1 4.77 us: outer_product(): lax.dot_general(basis, factor, (((1,), (1,)), ((), ())), precision=lax.Pr...]
  transfers between devices with their start and end apart: 2 -> 3, of which waited for: 2 -> 3; matrix products, arithmetic and copies ran while one was open for 0% -> 0% of each run, Pallas kernels for 0% -> 1%
where the time goes in v1:
time: 150 us
  blocking collectives  116 us (77%)
  starting transfers between devices  16.1 us (11%)
  Pallas kernels  8.48 us (6%)
  local copies, waits for them, and re-layouts  4.15 us (3%)
  waiting for transfers between devices  3.81 us (3%)
    all_to_all x7, blocking collectives, exchange(): return lax.all_to_all(blocks, axis, 0, 0, tiled=True)  116 us
    ppermute x1, starting transfers between devices, shards(): rest = lax.ppermute(total, 'c', swap)  6.98 us
    ppermute x1, starting transfers between devices, shards(): other = lax.ppermute(own, 'c', swap)  5.12 us
    ppermute x1, starting transfers between devices, shards(): away = lax.ppermute(away, 'c', swap)  4.03 us
    unnamed x14, local copies, waits for them, and re-layouts  3.25 us
  transfers between devices with their start and end apart: 3, of which 3 were waited for; matrix products, arithmetic and copies ran while one was open for 0% of the time, Pallas kernels for 1%

profile of v1, /device:TPU:1, one launch (start us, length us, event | category | flops | bytes accessed | tf_op | source)
XLA Modules:
  0.0 149.8 jit_solution(10370804413377147344)
XLA Ops:
  0.6 0.8 fusion
  1.5 0.1 pad.2.clone
  1.5 0.1 maximum_maximum_fusion
  1.6 27.1 %all_to_all.35.x_ref = f32[16,8,128]{2,1,0:T(8,128)S(1)} all-to-all(f32[16,8,128]{2,1,0:T(8,128)S(1)} %broadcast_in_dim.10), channel_id=1, replica_groups=mesh['zh'=8,'zl'=2,'s'=16,'c'=2] {'zh','zl'}, dimensions={0} | all-to-all | bytes 131072 | tf_op jit(solution)/shard_map/gather_q_prev/all_to_all | solution.py:168
  28.7 0.2 gather_q_prev.1
  28.9 17.2 %all_to_all.36.own_ref = f32[16,80,128]{2,1,0:T(8,128)S(1)} all-to-all(f32[16,80,128]{2,1,0:T(8,128)S(1)} %gather_q_prev.1), channel_id=1, replica_groups=mesh['zh'=8,'zl'=2,'s'=16,'c'=2] {'s'}, dimensions={0} | all-to-all | bytes 1310720 | tf_op jit(solution)/shard_map/gather_q_prev/all_to_all | solution.py:168
  46.1 5.1 %collective-permute-start = (f32[16,80,128]{2,1,0:T(8,128)S(1)}, f32[16,80,128]{2,1,0:T(8,128)S(1)}, u32[]{:S(2)}, u32[]{:S(2)}) collective-permute-start(f32[16,80,128]{2,1,0:T(8,128)S(1)} %all_to_all.36.own_ref), channel_id=1, source_target_pairs={{0,1},{1,0},{2,3},{3,2},{4,5},{5,4},{6,7},{7,6},{8,9},{9,8},{10,11... | collective-permute-start | bytes 1966088 | tf_op jit(solution)/shard_map/gather_q_prev/ppermute | solution.py:187
  51.3 1.7 %collective-permute-done.other_ref = f32[16,80,128]{2,1,0:T(8,128)S(1)} collective-permute-done((f32[16,80,128]{2,1,0:T(8,128)S(1)}, f32[16,80,128]{2,1,0:T(8,128)S(1)}, u32[]{:S(2)}, u32[]{:S(2)}) %collective-permute-start) | collective-permute-done | bytes 655392 | tf_op jit(solution)/shard_map/gather_q_prev/ppermute | solution.py:187
  53.0 0.8 copy-done.4
  53.8 1.3 copy-done.1
  55.1 1.1 copy-done.5
  56.2 1.1 left_factor.2
  57.3 11.1 %all_to_all.37.x_ref = f32[32,8,128]{2,1,0:T(8,128)S(1)} all-to-all(f32[32,8,128]{2,1,0:T(8,128)S(1)} %left_factor.2), channel_id=1, replica_groups=mesh['zh'=8,'zl'=2,'s'=16,'c'=2] {'s','c'}, dimensions={0} | all-to-all | bytes 262144 | tf_op jit(solution)/shard_map/left_factor/all_to_all | solution.py:168
  68.5 14.6 %all_to_all.38.tiles_ref = f32[16,8,128]{2,1,0:T(8,128)S(1)} all-to-all(f32[16,8,128]{2,1,0:T(8,128)S(1)} %left_factor.3), channel_id=1, replica_groups=mesh['zh'=8,'zl'=2,'s'=16,'c'=2] {'zh','zl'}, dimensions={0} | all-to-all | bytes 131072 | tf_op jit(solution)/shard_map/left_factor/all_to_all | solution.py:168
  83.1 2.8 %right_factor.4 = (f32[16,32]{1,0:T(8,128)S(1)}, f32[16,16,640]{2,1,0:T(8,128)S(1)}) custom-call(s32[1]{0:T(128)} %bitcast.c_ref, f32[16,8,128]{2,1,0:T(8,128)S(1)} %all_to_all.38.tiles_ref, bf16[32,20480]{1,0:T(8,128)(2,1)S(1)} %bitcast.17, bf16[32,20480]{1,0:T(8,128)(2,1)S(1)} %bitcast.21, s32[8,20480]{1,0:T(8,128)S(1)} %bitcast.26), custom_call_target="tpu_custom_call" | custom-call | tf_op jit(solution)/shard_map/right_factor/pallas_call | solution.py:215
  85.9 4.0 %collective-permute-start.1 = (f32[16,16,640]{2,1,0:T(8,128)S(1)}, f32[16,16,640]{2,1,0:T(8,128)S(1)}, u32[]{:S(2)}, u32[]{:S(2)}) collective-permute-start(f32[16,16,640]{2,1,0:T(8,128)S(1)} %get-tuple-element.7), channel_id=1, source_target_pairs={{0,1},{1,0},{2,3},{3,2},{4,5},{5,4},{6,7},{7,6},{8,9},{9,8},{10,11... | collective-permute-start | bytes 1966088 | tf_op jit(solution)/shard_map/right_factor/ppermute | solution.py:220
  89.9 1.3 right_factor.5
  91.3 0.4 collective-permute-done.1
  91.7 14.6 %all_to_all.39.x_ref = f32[32,8,640]{2,1,0:T(8,128)S(1)} all-to-all(f32[32,8,640]{2,1,0:T(8,128)S(1)} %bitcast.29), channel_id=1, replica_groups=mesh['zh'=8,'zl'=2,'s'=16,'c'=2] {'zl','s'}, dimensions={0} | all-to-all | bytes 1310720 | tf_op jit(solution)/shard_map/right_factor/all_to_all | solution.py:168
  106.4 17.3 %all_to_all.40.x_ref = f32[8,8,640]{2,1,0:T(8,128)S(1)} all-to-all(f32[8,8,640]{2,1,0:T(8,128)S(1)} %right_factor.6), channel_id=1, replica_groups=mesh['zh'=8,'zl'=2,'s'=16,'c'=2] {'zh'}, dimensions={0} | all-to-all | bytes 327680 | tf_op jit(solution)/shard_map/right_factor/all_to_all | solution.py:168
  123.8 14.3 %all_to_all.41 = f32[32,8,640]{2,1,0:T(8,128)S(1)} all-to-all(f32[32,8,640]{2,1,0:T(8,128)S(1)} %right_factor.7), channel_id=1, replica_groups=mesh['zh'=8,'zl'=2,'s'=16,'c'=2] {'zl','s'}, dimensions={0} | all-to-all | bytes 1310720 | tf_op jit(solution)/shard_map/right_factor/all_to_all | solution.py:168
  138.1 7.0 %collective-permute-start.2 = (f32[16,16,640]{2,1,0:T(8,128)S(1)}, f32[16,16,640]{2,1,0:T(8,128)}, u32[]{:S(2)}, u32[]{:S(2)}) collective-permute-start(f32[16,16,640]{2,1,0:T(8,128)S(1)} %bitcast.24), channel_id=1, source_target_pairs={{0,1},{1,0},{2,3},{3,2},{4,5},{5,4},{6,7},{7,6},{8,9},{9,8},{10,11... | collective-permute-start | bytes 1966088 | tf_op jit(solution)/shard_map/right_factor/ppermute | solution.py:228
  145.2 1.7 %collective-permute-done.2.other_ref = f32[16,16,640]{2,1,0:T(8,128)} collective-permute-done((f32[16,16,640]{2,1,0:T(8,128)S(1)}, f32[16,16,640]{2,1,0:T(8,128)}, u32[]{:S(2)}, u32[]{:S(2)}) %collective-permute-start.2) | collective-permute-done | bytes 655392 | tf_op jit(solution)/shard_map/right_factor/ppermute | solution.py:228
  146.9 3.0 %update.1 = (f32[16,40]{1,0:T(8,128)}, bf16[32,20480]{1,0:T(8,128)(2,1)}) custom-call(s32[3]{0:T(128)S(1)} %pad_add_fusion.where_ref, f32[16,32]{1,0:T(8,128)S(1)} %get-tuple-element.6.basis_ref, bf16[32,20480]{1,0:T(8,128)(2,1)S(1)} %bitcast.19, bf16[32,20480]{1,0:T(8,128)(2,1)S(1)} %bitcast.23, f32[16,16,640]{2,1,0:T(8,128)S(1)} %bitcast.25, ...), custom_call_target="tpu_custom_call" | custom-call | tf_op jit(solution)/shard_map/update/pallas_call | solution.py:231
  (18 shorter events, 0.3 us)
Async XLA Ops:
  0.6 53.2 %copy-start.6 = (s32[1,32,16]{1,2,0:T(8,128)S(1)}, s32[1,32,16]{1,2,0:T(8,128)}, u32[]{:S(2)}) copy-start(s32[1,32,16]{1,2,0:T(8,128)} %param.8) | copy-start | bytes 6148
  0.6 53.2 %copy-start = (bf16[1,32,20480]{2,1,0:T(8,128)(2,1)S(1)}, bf16[1,32,20480]{2,1,0:T(8,128)(2,1)}, u32[]{:S(2)}) copy-start(bf16[1,32,20480]{2,1,0:T(8,128)(2,1)} %param.5) | copy-start | bytes 3932164
  46.1 6.8 %collective-permute-start = (f32[16,80,128]{2,1,0:T(8,128)S(1)}, f32[16,80,128]{2,1,0:T(8,128)S(1)}, u32[]{:S(2)}, u32[]{:S(2)}) collective-permute-start(f32[16,80,128]{2,1,0:T(8,128)S(1)} %all_to_all.36.own_ref), channel_id=1, source_target_pairs={{0,1},{1,0},{2,3},{3,2},{4,5},{5,4},{6,7},{7,6},{8,9},{9,8},{10,11... | collective-permute-start | bytes 1966088 | tf_op jit(solution)/shard_map/gather_q_prev/ppermute | solution.py:187
  53.0 0.8 copy-start.4
  53.8 1.3 copy-start.1
  55.1 1.1 copy-start.5
  56.2 26.9 %copy-start.2 = (bf16[1,32,20480]{2,1,0:T(8,128)(2,1)S(1)}, bf16[1,32,20480]{2,1,0:T(8,128)(2,1)}, u32[]{:S(2)}) copy-start(bf16[1,32,20480]{2,1,0:T(8,128)(2,1)} %param.6) | copy-start | bytes 3932164
  56.2 26.9 %copy-start.3 = (s32[1,20480,8]{1,2,0:T(8,128)S(1)}, s32[1,20480,8]{1,2,0:T(8,128)}, u32[]{:S(2)}) copy-start(s32[1,20480,8]{1,2,0:T(8,128)} %param.9) | copy-start | bytes 1966084
  85.9 5.7 %collective-permute-start.1 = (f32[16,16,640]{2,1,0:T(8,128)S(1)}, f32[16,16,640]{2,1,0:T(8,128)S(1)}, u32[]{:S(2)}, u32[]{:S(2)}) collective-permute-start(f32[16,16,640]{2,1,0:T(8,128)S(1)} %get-tuple-element.7), channel_id=1, source_target_pairs={{0,1},{1,0},{2,3},{3,2},{4,5},{5,4},{6,7},{7,6},{8,9},{9,8},{10,11... | collective-permute-start | bytes 1966088 | tf_op jit(solution)/shard_map/right_factor/ppermute | solution.py:220
  138.1 8.8 %collective-permute-start.2 = (f32[16,16,640]{2,1,0:T(8,128)S(1)}, f32[16,16,640]{2,1,0:T(8,128)}, u32[]{:S(2)}, u32[]{:S(2)}) collective-permute-start(f32[16,16,640]{2,1,0:T(8,128)S(1)} %bitcast.24), channel_id=1, source_target_pairs={{0,1},{1,0},{2,3},{3,2},{4,5},{5,4},{6,7},{7,6},{8,9},{9,8},{10,11... | collective-permute-start | bytes 1966088 | tf_op jit(solution)/shard_map/right_factor/ppermute | solution.py:228

commit v2 on v1

--- a/solution.py
+++ b/solution.py
@@ -17,7 +17,7 @@
 WIDTH = 0.25
 F32 = jnp.float32
 BF16 = jnp.bfloat16
-VMEM_LIMIT = 48 * 1024 * 1024
+VMEM_LIMIT = 16 * 1024 * 1024
 
 
 def call(body, out_shape, **kw):
@@ -136,32 +136,39 @@
     store_blocks(sent, o_ref)
 
 
-def right_second(c_ref, basis_ref, grad_ref, res_ref, words_ref, o_ref):
+def right_second(c_ref, basis_ref, grad_ref, res_ref, words_ref, turned_ref, o_ref):
+    @pl.when(pl.program_id(0) == 0)
+    def _():
+        turned_ref[...] = basis_ref[...].T
+
     sent = right_columns(basis_ref[...], grad_ref[...], res_ref[...], words_ref[...])
     store_blocks(sent, o_ref)
 
 
-def update(where_ref, basis_ref, grad_ref, res_ref, own_ref, other_ref, q_ref, o_ref):
-    c, block, offset = where_ref[0], where_ref[1], where_ref[2]
-    high, low = parts(basis_ref[...].T, 2)
+def new_columns(turned_ref, grad_ref, res_ref, total_ref, o_ref):
+    high, low = parts(turned_ref[...], 2)
     left = jnp.concatenate([high, low, high], axis=1)
-
-    def columns(total_ref, base):
-        for t in range(HALF // BLOCK):
-            mean = total_ref[t] * (1.0 / WORLD)
-            mh, ml = parts(mean, 2)
-            right = jnp.concatenate([mh, mh, ml], axis=0)
-            approx = jnp.dot(left, right, preferred_element_type=F32)
-            at = pl.ds(pl.multiple_of(base + t * BLOCK, 128), BLOCK)
-            merged = grad_ref[:, at].astype(F32) + res_ref[:, at].astype(F32)
-            o_ref[:, at] = (merged - approx).astype(BF16)
-
-    columns(own_ref, c * HALF)
-    columns(other_ref, (1 - c) * HALF)
-    t = block % 16
-    mine = jnp.where(block // 16 == c, own_ref[t], other_ref[t])
-    mine = pltpu.roll(mine, (BLOCK - offset) % BLOCK, 1)
-    q_ref[...] = mine[:, 0:40] * WORLD ** (-0.5)
+    mean = jnp.concatenate([total_ref[t] for t in range(STEP // BLOCK)], axis=1) * (1.0 / WORLD)
+    mh, ml = parts(mean, 2)
+    right = jnp.concatenate([mh, mh, ml], axis=0)
+    approx = jnp.dot(left, right, preferred_element_type=F32)
+    merged = grad_ref[...].astype(F32) + res_ref[...].astype(F32)
+    o_ref[...] = (merged - approx).astype(BF16)
+
+
+def update_first(where_ref, turned_ref, grad_ref, res_ref, total_ref, o_ref):
+    new_columns(turned_ref, grad_ref, res_ref, total_ref, o_ref)
+
+
+def update_second(where_ref, turned_ref, grad_ref, res_ref, total_ref, own_ref, rest_ref, done_ref, q_ref, o_ref):
+    @pl.when(pl.program_id(0) == 0)
+    def _():
+        c, block, offset = where_ref[0], where_ref[1], where_ref[2]
+        mine = jnp.where(block // 16 == c, own_ref[0], rest_ref[0])
+        mine = pltpu.roll(mine, (BLOCK - offset) % BLOCK, 1)
+        q_ref[...] = mine[:, 0:40] * WORLD ** (-0.5)
+
+    new_columns(turned_ref, grad_ref, res_ref, total_ref, o_ref)
 
 
 def exchange(blocks, axis):
@@ -218,7 +225,11 @@
             grid_spec=grid((16, 8, 128), False, (pl.BlockSpec((16, 32), lambda i, c_ref: (0, 0)), blocks)),
         )(c.reshape(1), tile, grad, res, q_words)
         away = lax.ppermute(away, "c", swap)
-        kept = call(right_second, half, grid_spec=grid((16, 32), True, blocks))(c.reshape(1), basis, grad, res, q_words)
+        turned, kept = call(
+            right_second,
+            (jax.ShapeDtypeStruct((32, 16), F32), half),
+            grid_spec=grid((16, 32), True, (pl.BlockSpec((32, 16), lambda i, c_ref: (0, 0)), blocks)),
+        )(c.reshape(1), basis, grad, res, q_words)
         summed = (kept + away).reshape(32, 8, BLOCK)
         summed = exchange(summed, group)
         summed = call(add_and_repeat, jax.ShapeDtypeStruct((8, 8, BLOCK), F32), in_specs=[whole], out_specs=whole)(summed)
@@ -228,12 +239,38 @@
         rest = lax.ppermute(total, "c", swap)
     with jax.named_scope("update"):
         where = jnp.stack([c, device // 16, (device % 16) * 40])
+
+        def columns(side):
+            def place(i, w_ref):
+                return (0, (w_ref[0] if side else 1 - w_ref[0]) * steps + i)
+
+            return pl.BlockSpec((32, STEP), place)
+
+        fixed = pl.BlockSpec((32, 16), lambda i, w_ref: (0, 0))
+        blocks = pl.BlockSpec((STEP // BLOCK, 16, BLOCK), lambda i, w_ref: (i, 0, 0))
+        mine = pl.BlockSpec((1, 16, BLOCK), lambda i, w_ref: (w_ref[1] % 16, 0, 0))
+        done = jax.ShapeDtypeStruct((ROWS, FF), BF16)
+        updated = call(
+            update_first,
+            done,
+            grid_spec=pltpu.PrefetchScalarGridSpec(
+                num_scalar_prefetch=1,
+                grid=(steps,),
+                in_specs=[fixed, columns(True), columns(True), blocks],
+                out_specs=columns(True),
+            ),
+        )(where, turned, grad, res, total)
         q_next, updated = call(
-            update,
-            (jax.ShapeDtypeStruct((16, 40), F32), jax.ShapeDtypeStruct((ROWS, FF), BF16)),
-            in_specs=[scalars] + [whole] * 5,
-            out_specs=(whole, whole),
-        )(where, basis, grad, res, total, rest)
+            update_second,
+            (jax.ShapeDtypeStruct((16, 40), F32), done),
+            grid_spec=pltpu.PrefetchScalarGridSpec(
+                num_scalar_prefetch=1,
+                grid=(steps,),
+                in_specs=[fixed, columns(False), columns(False), blocks, mine, mine, pl.BlockSpec(memory_space=pl.ANY)],
+                out_specs=(pl.BlockSpec((16, 40), lambda i, w_ref: (0, 0)), columns(False)),
+            ),
+            input_output_aliases={7: 1},
+        )(where, turned, grad, res, rest, total, rest, updated)
     return (q_next.T, updated[None])
 
 

time: 150 us -> 153 us (1.020)
  Pallas kernels: 8.48 us -> 12.8 us
  waiting for transfers between devices: 3.81 us -> 1.97 us
    pallas_call x2 -> x3, Pallas kernels: 4.27 us -> 8.59 us  [the longest x1 4.41 us: shards(): call(update_second, (jax.ShapeDtypeStruct((16, 40), F32), done), grid_spe...]
    ppermute x1, waiting for transfers between devices: 1.73 us -> 0.01 us  [shards(): rest = lax.ppermute(total, 'c', swap)]
  transfers between devices with their start and end apart: 3 -> 3, of which waited for: 3 -> 2; matrix products, arithmetic and copies ran while one was open for 0% -> 0% of each run, Pallas kernels for 1% -> 3%
where the time goes in v2:
time: 153 us; the launch traced here: 152 us
  blocking collectives  116 us (76%)
  starting transfers between devices  16.1 us (11%)
  Pallas kernels  12.8 us (8%)
  local copies, waits for them, and re-layouts  4.15 us (3%)
  waiting for transfers between devices  1.97 us (1%)
    all_to_all x7, blocking collectives, exchange(): return lax.all_to_all(blocks, axis, 0, 0, tiled=True)  116 us
    ppermute x1, starting transfers between devices, shards(): rest = lax.ppermute(total, 'c', swap)  6.98 us
    ppermute x1, starting transfers between devices, shards(): other = lax.ppermute(own, 'c', swap)  5.12 us
    pallas_call x1, Pallas kernels, shards(): call(update_second, (jax.ShapeDtypeStruct((16, 40), F32), done), grid_spe...  4.41 us
    ppermute x1, starting transfers between devices, shards(): away = lax.ppermute(away, 'c', swap)  4.03 us
    unnamed x14, local copies, waits for them, and re-layouts  3.25 us
  transfers between devices with their start and end apart: 3, of which 2 were waited for; matrix products, arithmetic and copies ran while one was open for 0% of the time, Pallas kernels for 3%

profile of v2, /device:TPU:1, one launch (start us, length us, event | category | flops | bytes accessed | tf_op | source)
XLA Modules:
  0.0 152.3 jit_solution(14131846560681630793)
XLA Ops:
  0.6 0.8 fusion
  1.5 0.1 pad.2.clone
  1.5 0.1 maximum_maximum_fusion
  1.6 27.1 %all_to_all.35.x_ref = f32[16,8,128]{2,1,0:T(8,128)S(1)} all-to-all(f32[16,8,128]{2,1,0:T(8,128)S(1)} %broadcast_in_dim.10), channel_id=1, replica_groups=mesh['zh'=8,'zl'=2,'s'=16,'c'=2] {'zh','zl'}, dimensions={0} | all-to-all | bytes 131072 | tf_op jit(solution)/shard_map/gather_q_prev/all_to_all | solution.py:175
  28.7 0.2 gather_q_prev.1
  28.9 17.2 %all_to_all.36.own_ref = f32[16,80,128]{2,1,0:T(8,128)S(1)} all-to-all(f32[16,80,128]{2,1,0:T(8,128)S(1)} %gather_q_prev.1), channel_id=1, replica_groups=mesh['zh'=8,'zl'=2,'s'=16,'c'=2] {'s'}, dimensions={0} | all-to-all | bytes 1310720 | tf_op jit(solution)/shard_map/gather_q_prev/all_to_all | solution.py:175
  46.1 5.1 %collective-permute-start = (f32[16,80,128]{2,1,0:T(8,128)S(1)}, f32[16,80,128]{2,1,0:T(8,128)S(1)}, u32[]{:S(2)}, u32[]{:S(2)}) collective-permute-start(f32[16,80,128]{2,1,0:T(8,128)S(1)} %all_to_all.36.own_ref), channel_id=1, source_target_pairs={{0,1},{1,0},{2,3},{3,2},{4,5},{5,4},{6,7},{7,6},{8,9},{9,8},{10,11... | collective-permute-start | bytes 1966088 | tf_op jit(solution)/shard_map/gather_q_prev/ppermute | solution.py:194
  51.3 1.7 %collective-permute-done.other_ref = f32[16,80,128]{2,1,0:T(8,128)S(1)} collective-permute-done((f32[16,80,128]{2,1,0:T(8,128)S(1)}, f32[16,80,128]{2,1,0:T(8,128)S(1)}, u32[]{:S(2)}, u32[]{:S(2)}) %collective-permute-start) | collective-permute-done | bytes 655392 | tf_op jit(solution)/shard_map/gather_q_prev/ppermute | solution.py:194
  53.0 0.8 copy-done.4
  53.8 1.3 copy-done.1
  55.1 1.1 copy-done.5
  56.2 1.1 left_factor.2
  57.3 11.1 %all_to_all.37.x_ref = f32[32,8,128]{2,1,0:T(8,128)S(1)} all-to-all(f32[32,8,128]{2,1,0:T(8,128)S(1)} %left_factor.2), channel_id=1, replica_groups=mesh['zh'=8,'zl'=2,'s'=16,'c'=2] {'s','c'}, dimensions={0} | all-to-all | bytes 262144 | tf_op jit(solution)/shard_map/left_factor/all_to_all | solution.py:175
  68.5 14.6 %all_to_all.38.tiles_ref = f32[16,8,128]{2,1,0:T(8,128)S(1)} all-to-all(f32[16,8,128]{2,1,0:T(8,128)S(1)} %left_factor.3), channel_id=1, replica_groups=mesh['zh'=8,'zl'=2,'s'=16,'c'=2] {'zh','zl'}, dimensions={0} | all-to-all | bytes 131072 | tf_op jit(solution)/shard_map/left_factor/all_to_all | solution.py:175
  83.1 2.8 %right_factor.4 = (f32[16,32]{1,0:T(8,128)S(1)}, f32[16,16,640]{2,1,0:T(8,128)S(1)}) custom-call(s32[1]{0:T(128)} %bitcast.c_ref, f32[16,8,128]{2,1,0:T(8,128)S(1)} %all_to_all.38.tiles_ref, bf16[32,20480]{1,0:T(8,128)(2,1)S(1)} %bitcast.17, bf16[32,20480]{1,0:T(8,128)(2,1)S(1)} %bitcast.22, s32[8,20480]{1,0:T(8,128)S(1)} %bitcast.29), custom_call_target="tpu_custom_call" | custom-call | tf_op jit(solution)/shard_map/right_factor/pallas_call | solution.py:222
  85.9 4.0 %collective-permute-start.1 = (f32[16,16,640]{2,1,0:T(8,128)S(1)}, f32[16,16,640]{2,1,0:T(8,128)S(1)}, u32[]{:S(2)}, u32[]{:S(2)}) collective-permute-start(f32[16,16,640]{2,1,0:T(8,128)S(1)} %get-tuple-element.11), channel_id=1, source_target_pairs={{0,1},{1,0},{2,3},{3,2},{4,5},{5,4},{6,7},{7,6},{8,9},{9,8},{10,11... | collective-permute-start | bytes 1966088 | tf_op jit(solution)/shard_map/right_factor/ppermute | solution.py:227
  89.9 1.4 right_factor.5
  91.4 0.3 collective-permute-done.1
  91.7 14.6 %all_to_all.39.x_ref = f32[32,8,640]{2,1,0:T(8,128)S(1)} all-to-all(f32[32,8,640]{2,1,0:T(8,128)S(1)} %bitcast.33), channel_id=1, replica_groups=mesh['zh'=8,'zl'=2,'s'=16,'c'=2] {'zl','s'}, dimensions={0} | all-to-all | bytes 1310720 | tf_op jit(solution)/shard_map/right_factor/all_to_all | solution.py:175
  106.4 17.3 %all_to_all.40.x_ref = f32[8,8,640]{2,1,0:T(8,128)S(1)} all-to-all(f32[8,8,640]{2,1,0:T(8,128)S(1)} %right_factor.6), channel_id=1, replica_groups=mesh['zh'=8,'zl'=2,'s'=16,'c'=2] {'zh'}, dimensions={0} | all-to-all | bytes 327680 | tf_op jit(solution)/shard_map/right_factor/all_to_all | solution.py:175
  123.8 14.3 %all_to_all.41 = f32[32,8,640]{2,1,0:T(8,128)S(1)} all-to-all(f32[32,8,640]{2,1,0:T(8,128)S(1)} %right_factor.7), channel_id=1, replica_groups=mesh['zh'=8,'zl'=2,'s'=16,'c'=2] {'zl','s'}, dimensions={0} | all-to-all | bytes 1310720 | tf_op jit(solution)/shard_map/right_factor/all_to_all | solution.py:175
  138.1 7.0 %collective-permute-start.2 = (f32[16,16,640]{2,1,0:T(8,128)S(1)}, f32[16,16,640]{2,1,0:T(8,128)}, u32[]{:S(2)}, u32[]{:S(2)}) collective-permute-start(f32[16,16,640]{2,1,0:T(8,128)S(1)} %bitcast.26), channel_id=1, source_target_pairs={{0,1},{1,0},{2,3},{3,2},{4,5},{5,4},{6,7},{7,6},{8,9},{9,8},{10,11... | collective-permute-start | bytes 1966088 | tf_op jit(solution)/shard_map/right_factor/ppermute | solution.py:239
  145.2 2.8 %update.2.done_ref = bf16[32,20480]{1,0:T(8,128)(2,1)} custom-call(s32[3]{0:T(128)S(1)} %pad_add_fusion.where_ref, f32[32,16]{1,0:T(8,128)S(1)} %get-tuple-element.9.turned_ref, bf16[32,20480]{1,0:T(8,128)(2,1)S(1)} %bitcast.19, bf16[32,20480]{1,0:T(8,128)(2,1)S(1)} %bitcast.24, f32[16,16,640]{2,1,0:T(8,128)S(1)} %bitcast.27), custom_call_target="tpu_custom_call" | custom-call | tf_op jit(solution)/shard_map/update/pallas_call | solution.py:253
  147.9 4.4 %update.3 = (f32[16,40]{1,0:T(8,128)}, bf16[32,20480]{1,0:T(8,128)(2,1)}) custom-call(s32[3]{0:T(128)S(1)} %pad_add_fusion.where_ref, f32[32,16]{1,0:T(8,128)S(1)} %get-tuple-element.9.turned_ref, bf16[32,20480]{1,0:T(8,128)(2,1)S(1)} %bitcast.20, bf16[32,20480]{1,0:T(8,128)(2,1)S(1)} %bitcast.25, ...), custom_call_target="tpu_custom_call", output_to_operand_aliasing={{1}: (7, {})} | custom-call | tf_op jit(solution)/shard_map/update/pallas_call | solution.py:263
  (19 shorter events, 0.3 us)
Async XLA Ops:
  0.6 53.2 %copy-start.6 = (s32[1,32,16]{1,2,0:T(8,128)S(1)}, s32[1,32,16]{1,2,0:T(8,128)}, u32[]{:S(2)}) copy-start(s32[1,32,16]{1,2,0:T(8,128)} %param.8) | copy-start | bytes 6148
  0.6 53.2 %copy-start = (bf16[1,32,20480]{2,1,0:T(8,128)(2,1)S(1)}, bf16[1,32,20480]{2,1,0:T(8,128)(2,1)}, u32[]{:S(2)}) copy-start(bf16[1,32,20480]{2,1,0:T(8,128)(2,1)} %param.5) | copy-start | bytes 3932164
  46.1 6.8 %collective-permute-start = (f32[16,80,128]{2,1,0:T(8,128)S(1)}, f32[16,80,128]{2,1,0:T(8,128)S(1)}, u32[]{:S(2)}, u32[]{:S(2)}) collective-permute-start(f32[16,80,128]{2,1,0:T(8,128)S(1)} %all_to_all.36.own_ref), channel_id=1, source_target_pairs={{0,1},{1,0},{2,3},{3,2},{4,5},{5,4},{6,7},{7,6},{8,9},{9,8},{10,11... | collective-permute-start | bytes 1966088 | tf_op jit(solution)/shard_map/gather_q_prev/ppermute | solution.py:194
  53.0 0.8 copy-start.4
  53.8 1.3 copy-start.1
  55.1 1.1 copy-start.5
  56.2 26.9 %copy-start.2 = (bf16[1,32,20480]{2,1,0:T(8,128)(2,1)S(1)}, bf16[1,32,20480]{2,1,0:T(8,128)(2,1)}, u32[]{:S(2)}) copy-start(bf16[1,32,20480]{2,1,0:T(8,128)(2,1)} %param.6) | copy-start | bytes 3932164
  56.2 26.9 %copy-start.3 = (s32[1,20480,8]{1,2,0:T(8,128)S(1)}, s32[1,20480,8]{1,2,0:T(8,128)}, u32[]{:S(2)}) copy-start(s32[1,20480,8]{1,2,0:T(8,128)} %param.9) | copy-start | bytes 1966084
  85.9 5.7 %collective-permute-start.1 = (f32[16,16,640]{2,1,0:T(8,128)S(1)}, f32[16,16,640]{2,1,0:T(8,128)S(1)}, u32[]{:S(2)}, u32[]{:S(2)}) collective-permute-start(f32[16,16,640]{2,1,0:T(8,128)S(1)} %get-tuple-element.11), channel_id=1, source_target_pairs={{0,1},{1,0},{2,3},{3,2},{4,5},{5,4},{6,7},{7,6},{8,9},{9,8},{10,11... | collective-permute-start | bytes 1966088 | tf_op jit(solution)/shard_map/right_factor/ppermute | solution.py:227
  138.1 9.9 %collective-permute-start.2 = (f32[16,16,640]{2,1,0:T(8,128)S(1)}, f32[16,16,640]{2,1,0:T(8,128)}, u32[]{:S(2)}, u32[]{:S(2)}) collective-permute-start(f32[16,16,640]{2,1,0:T(8,128)S(1)} %bitcast.26), channel_id=1, source_target_pairs={{0,1},{1,0},{2,3},{3,2},{4,5},{5,4},{6,7},{7,6},{8,9},{9,8},{10,11... | collective-permute-start | bytes 1966088 | tf_op jit(solution)/shard_map/right_factor/ppermute | solution.py:239

commit v3 on v1

v3 whole, which is shorter than its diff:
```python
import functools

import jax
import jax.numpy as jnp
from jax import lax
from jax.experimental import pallas as pl
from jax.experimental.pallas import tpu as pltpu
from jax.sharding import Mesh, PartitionSpec as P

FF = 20480
RANK = 16
ROWS = 32
WORLD = 512
HALF = FF // 2
BLOCK = 640
STEP = 2560
WIDTH = 0.25
F32 = jnp.float32
BF16 = jnp.bfloat16
VMEM_LIMIT = 16 * 1024 * 1024


def call(body, out_shape, **kw):
    return pl.pallas_call(
        body,
        out_shape=out_shape,
        compiler_params=pltpu.CompilerParams(vmem_limit_bytes=VMEM_LIMIT),
        **kw,
    )


def parts(x, n):
    out = []
    for _ in range(n):
        p = x.astype(BF16)
        out.append(p)
        x = x - p.astype(F32)
    return out


def pack_factor(q_ref, o_ref):
    flat = jnp.concatenate([q_ref[r : r + 1, :] for r in range(RANK)], axis=1)
    for z in range(o_ref.shape[0]):
        o_ref[z] = flat


def spread_factor(x_ref, o_ref):
    pieces = x_ref[:, 0, :]
    halves = []
    for g in range(2):
        rows = [pieces[g * 8 : g * 8 + 8, r * 40 : r * 40 + 40] for r in range(RANK)]
        halves.append(jnp.concatenate(rows, axis=0).T)
    packed = jnp.concatenate(halves, axis=0)
    for s in range(o_ref.shape[0]):
        o_ref[s] = packed


def left_factor(c_ref, grad_ref, res_ref, own_ref, other_ref, bits_ref, o_ref):
    c = c_ref[0]
    lane = lax.broadcasted_iota(jnp.int32, (ROWS, 128), 1)
    owner = lane % 8
    total = jnp.zeros((ROWS, 128), F32)
    for g in range(2):
        chunks = []
        for s in range(16):
            a = own_ref[s, g * 40 : g * 40 + 40, :]
            b = other_ref[s, g * 40 : g * 40 + 40, :]
            chunks.append(jnp.where(c == 0, a, b))
            chunks.append(jnp.where(c == 0, b, a))
        factor = jnp.concatenate(chunks, axis=0)
        factor = jnp.concatenate(parts(factor, 2), axis=1)
        rows = [ref[:, z * 1280 : z * 1280 + 1280] for ref in (grad_ref, res_ref) for z in range(g * 8, g * 8 + 8)]
        prod = jnp.dot(jnp.concatenate(rows, axis=0), factor, preferred_element_type=F32)
        prod = prod[0:256] + prod[256:512]
        prod = prod[:, 0:128] + prod[:, 128:256]
        for e in range(8):
            total = total + jnp.where(owner == e, prod[e * 32 : e * 32 + 32], 0.0)
    rank = lax.broadcasted_iota(jnp.int32, (RANK, 128), 0)
    lane = lax.broadcasted_iota(jnp.int32, (RANK, 128), 1)
    fold = jnp.where(lane // 8 == rank, 1.0, 0.0).astype(F32)
    local = lax.dot_general(
        fold, total, (((1,), (1,)), ((), ())), precision=lax.Precision.HIGHEST, preferred_element_type=F32
    )
    noise = bits_ref[...].astype(F32) * 2.0 ** (-21) - 0.5
    sent = (local + noise * WIDTH * jnp.abs(local)).astype(BF16).astype(F32)
    tile = jnp.concatenate([sent[r : r + 4] for r in range(0, RANK, 4)], axis=1)
    for s in range(o_ref.shape[0]):
        o_ref[s] = tile


def add_and_repeat(x_ref, o_ref):
    total = x_ref[0]
    for s in range(1, x_ref.shape[0]):
        total = total + x_ref[s]
    for s in range(o_ref.shape[0]):
        o_ref[s] = total


def orthonormal(rows):
    index = lax.broadcasted_iota(jnp.int32, (RANK, 1), 0)
    for j in range(RANK):
        vector = rows[j : j + 1]
        inner = jnp.sum(rows * vector, axis=1, keepdims=True)
        square = inner[j : j + 1]
        unit = vector * lax.rsqrt(square)
        later = jnp.where(index > j, inner / square, 0.0)
        rows = jnp.where(index == j, unit, rows - later * vector)
    return rows


def right_columns(basis, grad, res, words):
    split = jnp.concatenate(parts(basis, 3), axis=0)
    split = jnp.concatenate([split, split], axis=1)
    both = jnp.concatenate([grad, res], axis=0)
    prod = jnp.dot(split, both, preferred_element_type=F32)
    local = prod[0:16] + prod[16:32] + prod[32:48]
    low = (words & 127).astype(F32) * (1.0 / 128.0)
    high = (words >> 7).astype(F32) * (1.0 / 64.0)
    noise = jnp.concatenate([low, high], axis=0) - 0.5
    return (local + noise * WIDTH * jnp.abs(local)).astype(BF16).astype(F32)


def half_columns(side, basis, grad_ref, res_ref, words_ref, o_ref):
    for i in range(HALF // STEP):
        at = pl.ds(pl.multiple_of(side * HALF + i * STEP, STEP), STEP)
        sent = right_columns(basis, grad_ref[:, at], res_ref[:, at], words_ref[:, at])
        for t in range(STEP // BLOCK):
            o_ref[i * (STEP // BLOCK) + t] = sent[:, t * BLOCK : t * BLOCK + BLOCK]


def right_first(c_ref, tiles_ref, grad_ref, res_ref, words_ref, basis_ref, o_ref):
    total = tiles_ref[0]
    for s in range(1, tiles_ref.shape[0]):
        total = total + tiles_ref[s]
    rows = jnp.concatenate([total[:, r : r + 32] for r in range(0, 128, 32)], axis=0)
    basis = orthonormal(rows)
    basis_ref[...] = basis
    half_columns(1 - c_ref[0], basis, grad_ref, res_ref, words_ref, o_ref)


def right_second(c_ref, basis_ref, grad_ref, res_ref, words_ref, turned_ref, o_ref):
    turned_ref[...] = basis_ref[...].T
    half_columns(c_ref[0], basis_ref[...], grad_ref, res_ref, words_ref, o_ref)


def new_columns(side, turned_ref, grad_ref, res_ref, total_ref, o_ref, made_ref, sems):
    high, low = parts(turned_ref[...] * (1.0 / WORLD), 2)
    left = jnp.concatenate([high, low, high], axis=1)
    copies = []
    for i in range(HALF // STEP):
        at = pl.ds(pl.multiple_of(side * HALF + i * STEP, STEP), STEP)
        here = pl.ds(i * STEP, STEP)
        blocks = [total_ref[t] for t in range(i * STEP // BLOCK, (i + 1) * STEP // BLOCK)]
        th, tl = parts(jnp.concatenate(blocks, axis=1), 2)
        right = jnp.concatenate([th, th, tl], axis=0)
        approx = jnp.dot(left, right, preferred_element_type=F32)
        merged = grad_ref[:, at].astype(F32) + res_ref[:, at].astype(F32)
        made_ref[:, here] = (merged - approx).astype(BF16)
        copy = pltpu.make_async_copy(made_ref.at[:, here], o_ref.at[:, at], sems.at[i])
        copy.start()
        copies.append(copy)
    return copies


def update_first(where_ref, turned_ref, grad_ref, res_ref, own_ref, o_ref, made_ref, sems):
    for copy in new_columns(where_ref[0], turned_ref, grad_ref, res_ref, own_ref, o_ref, made_ref, sems):
        copy.wait()


def update_second(
    where_ref, turned_ref, grad_ref, res_ref, own_ref, rest_ref, done_ref, q_ref, o_ref, made_ref, sems
):
    c, block, offset = where_ref[0], where_ref[1], where_ref[2]
    copies = new_columns(1 - c, turned_ref, grad_ref, res_ref, rest_ref, o_ref, made_ref, sems)
    t = block % 16
    mine = jnp.where(block // 16 == c, own_ref[t], rest_ref[t])
    mine = pltpu.roll(mine, (BLOCK - offset) % BLOCK, 1)
    q_ref[...] = mine[:, 0:40] * WORLD ** (-0.5)
    for copy in copies:
        copy.wait()


def exchange(blocks, axis):
    return lax.all_to_all(blocks, axis, 0, 0, tiled=True)


def shards(gradient, residual, q_prev, p_bits, q_bits):
    z, plane, group = ("zh", "zl"), ("s", "c"), ("zl", "s")
    grad, res = gradient[0], residual[0]
    p_words, q_words = p_bits[0].T, q_bits[0].T
    c = lax.axis_index("c")
    device = lax.axis_index(("zh", "zl", "s", "c"))
    swap = [(0, 1), (1, 0)]
    whole = pl.BlockSpec(memory_space=pltpu.VMEM)
    far = pl.BlockSpec(memory_space=pl.ANY)
    scalars = pl.BlockSpec(memory_space=pltpu.SMEM)

    with jax.named_scope("gather_q_prev"):
        pieces = call(pack_factor, jax.ShapeDtypeStruct((16, 1, 640), F32), in_specs=[whole], out_specs=whole)(q_prev.T)
        pieces = exchange(pieces, z)
        spread = call(
            spread_factor,
            jax.ShapeDtypeStruct((16, 80, 128), F32),
            in_specs=[whole],
            out_specs=whole,
            cost_estimate=pl.CostEstimate(flops=10**11, bytes_accessed=10**8, transcendentals=0),
        )(pieces)
        own = exchange(spread, "s")
        other = lax.ppermute(own, "c", swap)
    with jax.named_scope("left_factor"):
        tile = call(
            left_factor,
            jax.ShapeDtypeStruct((32, 4, 128), F32),
            in_specs=[scalars] + [whole] * 5,
            out_specs=whole,
        )(c.reshape(1), grad, res, own, other, p_words)
        tile = exchange(tile, plane)
        tile = call(add_and_repeat, jax.ShapeDtypeStruct((16, 4, 128), F32), in_specs=[whole], out_specs=whole)(tile)
        tile = exchange(tile, z)
    steps = HALF // STEP
    with jax.named_scope("right_factor"):
        half = jax.ShapeDtypeStruct((16, 16, BLOCK), F32)
        basis, away = call(
            right_first,
            (jax.ShapeDtypeStruct((16, 32), F32), half),
            in_specs=[scalars] + [whole] * 4,
            out_specs=(whole, whole),
        )(c.reshape(1), tile, grad, res, q_words)
        away = lax.ppermute(away, "c", swap)
        turned, kept = call(
            right_second,
            (jax.ShapeDtypeStruct((32, 16), F32), half),
            in_specs=[scalars] + [whole] * 4,
            out_specs=(whole, whole),
        )(c.reshape(1), basis, grad, res, q_words)
        summed = (kept + away).reshape(32, 8, BLOCK)
        summed = exchange(summed, group)
        summed = call(add_and_repeat, jax.ShapeDtypeStruct((8, 8, BLOCK), F32), in_specs=[whole], out_specs=whole)(summed)
        summed = exchange(summed, "zh")
        summed = call(add_and_repeat, jax.ShapeDtypeStruct((32, 8, BLOCK), F32), in_specs=[whole], out_specs=whole)(summed)
        total = exchange(summed, group).reshape(16, 16, BLOCK)
        rest = lax.ppermute(total, "c", swap)
    with jax.named_scope("update"):
        where = jnp.stack([c, device // 16, (device % 16) * 40])
        done = jax.ShapeDtypeStruct((ROWS, FF), BF16)
        room = [pltpu.VMEM((ROWS, HALF), BF16), pltpu.SemaphoreType.DMA((steps,))]
        updated = call(
            update_first, done, in_specs=[scalars] + [whole] * 4, out_specs=far, scratch_shapes=room
        )(where, turned, grad, res, total)
        q_next, updated = call(
            update_second,
            (jax.ShapeDtypeStruct((16, 40), F32), done),
            in_specs=[scalars] + [whole] * 5 + [far],
            out_specs=(whole, far),
            scratch_shapes=room,
            input_output_aliases={6: 1},
        )(where, turned, grad, res, total, rest, updated)
    return (q_next.T, updated[None])


def solution(mesh):
    every = ("zh", "zl", "s", "c")
    split = Mesh(mesh.devices.reshape(8, 2, 16, 2), every)
    row, block = P(every, None), P(every, None, None)
    return jax.shard_map(
        shards,
        mesh=split,
        in_specs=(block, block, row, block, block),
        out_specs=(row, block),
        check_vma=False,
    )
```

time: 150 us -> 146 us (0.973)
  local copies, waits for them, and re-layouts: 4.15 us -> 0.71 us
    unnamed x14 -> x10, local copies, waits for them, and re-layouts: 3.25 us -> 0.71 us
    ppermute x1, waiting for transfers between devices: 1.73 us -> 0.04 us  [shards(): rest = lax.ppermute(total, 'c', swap)]
    pallas_call x5 -> x7, Pallas kernels: 8.19 us -> 9.53 us  [the longest x1 2.83 us: shards(): call(update_second, (jax.ShapeDtypeStruct((16, 40), F32), done), in_specs...]
  transfers between devices with their start and end apart: 3 -> 3, of which waited for: 3 -> 2; matrix products, arithmetic and copies ran while one was open for 0% -> 0% of each run, Pallas kernels for 1% -> 2%
where the time goes in v3:
time: 146 us; the launch traced here: 145 us
  blocking collectives  115 us (79%)
  starting transfers between devices  15.6 us (11%)
  Pallas kernels  9.82 us (7%)
  waiting for transfers between devices  3 us (2%)
    all_to_all x7, blocking collectives, exchange(): return lax.all_to_all(blocks, axis, 0, 0, tiled=True)  115 us
    ppermute x1, starting transfers between devices, shards(): rest = lax.ppermute(total, 'c', swap)  6.98 us
    ppermute x1, starting transfers between devices, shards(): other = lax.ppermute(own, 'c', swap)  5.07 us
    ppermute x1, starting transfers between devices, shards(): away = lax.ppermute(away, 'c', swap)  3.57 us
  transfers between devices with their start and end apart: 3, of which 2 were waited for; matrix products, arithmetic and copies ran while one was open for 0% of the time, Pallas kernels for 2%

profile of v3, /device:TPU:1, one launch (start us, length us, event | category | flops | bytes accessed | tf_op | source)
XLA Modules:
  0.0 145.1 jit_solution(14872997261765927912)
XLA Ops:
  0.6 0.7 copy-done.4
  1.3 0.1 gather_q_prev.2
  1.4 27.1 %all_to_all.35.x_ref = f32[16,1,640]{2,1,0:T(1,128)S(1)} all-to-all(f32[16,1,640]{2,1,0:T(1,128)S(1)} %gather_q_prev.2), channel_id=1, replica_groups=mesh['zh'=8,'zl'=2,'s'=16,'c'=2] {'zh','zl'}, dimensions={0} | all-to-all | bytes 81920 | tf_op jit(solution)/shard_map/gather_q_prev/all_to_all | solution.py:184
  28.5 0.2 gather_q_prev.3
  28.7 17.4 %all_to_all.36.own_ref = f32[16,80,128]{2,1,0:T(8,128)S(1)} all-to-all(f32[16,80,128]{2,1,0:T(8,128)S(1)} %gather_q_prev.3), channel_id=1, replica_groups=mesh['zh'=8,'zl'=2,'s'=16,'c'=2] {'s'}, dimensions={0} | all-to-all | bytes 1310720 | tf_op jit(solution)/shard_map/gather_q_prev/all_to_all | solution.py:184
  46.1 5.1 %collective-permute-start = (f32[16,80,128]{2,1,0:T(8,128)S(1)}, f32[16,80,128]{2,1,0:T(8,128)}, u32[]{:S(2)}, u32[]{:S(2)}) collective-permute-start(f32[16,80,128]{2,1,0:T(8,128)S(1)} %all_to_all.36.own_ref), channel_id=1, source_target_pairs={{0,1},{1,0},{2,3},{3,2},{4,5},{5,4},{6,7},{7,6},{8,9},{9,8},{10,11... | collective-permute-start | bytes 1966088 | tf_op jit(solution)/shard_map/gather_q_prev/ppermute | solution.py:209
  51.2 1.8 %collective-permute-done.other_ref = f32[16,80,128]{2,1,0:T(8,128)} collective-permute-done((f32[16,80,128]{2,1,0:T(8,128)S(1)}, f32[16,80,128]{2,1,0:T(8,128)}, u32[]{:S(2)}, u32[]{:S(2)}) %collective-permute-start) | collective-permute-done | bytes 655392 | tf_op jit(solution)/shard_map/gather_q_prev/ppermute | solution.py:209
  53.0 2.2 %left_factor.2 = f32[32,4,128]{2,1,0:T(4,128)S(1)} custom-call(s32[1]{0:T(128)} %bitcast.c_ref, bf16[32,20480]{1,0:T(8,128)(2,1)S(1)} %bitcast.16, bf16[32,20480]{1,0:T(8,128)(2,1)S(1)} %bitcast.21, f32[16,80,128]{2,1,0:T(8,128)S(1)} %all_to_all.36.own_ref, f32[16,80,128]{2,1,0:T(8,128)} %collective-permute-done.other_ref, s32[16,32]{1,0:T(8,128)S(1)} %bitcast.31), custom_call_target="tpu_custom_call" | custom-call | tf_op jit(solution)/shard_map/left_factor/pallas_call | solution.py:211
  55.3 10.8 %all_to_all.37.x_ref = f32[32,4,128]{2,1,0:T(4,128)S(1)} all-to-all(f32[32,4,128]{2,1,0:T(4,128)S(1)} %left_factor.2), channel_id=1, replica_groups=mesh['zh'=8,'zl'=2,'s'=16,'c'=2] {'s','c'}, dimensions={0} | all-to-all | bytes 131072 | tf_op jit(solution)/shard_map/left_factor/all_to_all | solution.py:184
  66.1 14.0 %all_to_all.38.tiles_ref = f32[16,4,128]{2,1,0:T(4,128)S(1)} all-to-all(f32[16,4,128]{2,1,0:T(4,128)S(1)} %left_factor.3), channel_id=1, replica_groups=mesh['zh'=8,'zl'=2,'s'=16,'c'=2] {'zh','zl'}, dimensions={0} | all-to-all | bytes 65536 | tf_op jit(solution)/shard_map/left_factor/all_to_all | solution.py:184
  80.1 2.1 %right_factor.4 = (f32[16,32]{1,0:T(8,128)S(1)}, f32[16,16,640]{2,1,0:T(8,128)S(1)}) custom-call(s32[1]{0:T(128)} %bitcast.c_ref, f32[16,4,128]{2,1,0:T(4,128)S(1)} %all_to_all.38.tiles_ref, bf16[32,20480]{1,0:T(8,128)(2,1)S(1)} %bitcast.17, bf16[32,20480]{1,0:T(8,128)(2,1)S(1)} %bitcast.22, s32[8,20480]{1,0:T(8,128)S(1)} %bitcast.29), custom_call_target="tpu_custom_call" | custom-call | tf_op jit(solution)/shard_map/right_factor/pallas_call | solution.py:223
  82.2 3.6 %collective-permute-start.1 = (f32[16,16,640]{2,1,0:T(8,128)S(1)}, f32[16,16,640]{2,1,0:T(8,128)S(1)}, u32[]{:S(2)}, u32[]{:S(2)}) collective-permute-start(f32[16,16,640]{2,1,0:T(8,128)S(1)} %get-tuple-element.11), channel_id=1, source_target_pairs={{0,1},{1,0},{2,3},{3,2},{4,5},{5,4},{6,7},{7,6},{8,9},{9,8},{10,11... | collective-permute-start | bytes 1966088 | tf_op jit(solution)/shard_map/right_factor/ppermute | solution.py:229
  85.8 0.6 right_factor.5
  86.4 1.1 collective-permute-done.1
  87.5 0.1 add.21
  87.6 14.4 %all_to_all.39.x_ref = f32[32,8,640]{2,1,0:T(8,128)S(1)} all-to-all(f32[32,8,640]{2,1,0:T(8,128)S(1)} %bitcast.34), channel_id=1, replica_groups=mesh['zh'=8,'zl'=2,'s'=16,'c'=2] {'zl','s'}, dimensions={0} | all-to-all | bytes 1310720 | tf_op jit(solution)/shard_map/right_factor/all_to_all | solution.py:184
  102.0 0.1 right_factor.6
  102.0 17.1 %all_to_all.40.x_ref = f32[8,8,640]{2,1,0:T(8,128)S(1)} all-to-all(f32[8,8,640]{2,1,0:T(8,128)S(1)} %right_factor.6), channel_id=1, replica_groups=mesh['zh'=8,'zl'=2,'s'=16,'c'=2] {'zh'}, dimensions={0} | all-to-all | bytes 327680 | tf_op jit(solution)/shard_map/right_factor/all_to_all | solution.py:184
  119.1 0.1 right_factor.7
  119.2 14.3 %all_to_all.41 = f32[32,8,640]{2,1,0:T(8,128)S(1)} all-to-all(f32[32,8,640]{2,1,0:T(8,128)S(1)} %right_factor.7), channel_id=1, replica_groups=mesh['zh'=8,'zl'=2,'s'=16,'c'=2] {'zl','s'}, dimensions={0} | all-to-all | bytes 1310720 | tf_op jit(solution)/shard_map/right_factor/all_to_all | solution.py:184
  133.5 7.0 %collective-permute-start.2 = (f32[16,16,640]{2,1,0:T(8,128)S(1)}, f32[16,16,640]{2,1,0:T(8,128)}, u32[]{:S(2)}, u32[]{:S(2)}) collective-permute-start(f32[16,16,640]{2,1,0:T(8,128)S(1)} %bitcast.26), channel_id=1, source_target_pairs={{0,1},{1,0},{2,3},{3,2},{4,5},{5,4},{6,7},{7,6},{8,9},{9,8},{10,11... | collective-permute-start | bytes 1966088 | tf_op jit(solution)/shard_map/right_factor/ppermute | solution.py:242
  140.5 0.1 pad_add_fusion.where_ref
  140.6 1.7 %update.2.done_ref = bf16[32,20480]{1,0:T(8,128)(2,1)} custom-call(s32[3]{0:T(128)S(1)} %pad_add_fusion.where_ref, f32[32,16]{1,0:T(8,128)S(1)} %get-tuple-element.9.turned_ref, bf16[32,20480]{1,0:T(8,128)(2,1)S(1)} %bitcast.19, bf16[32,20480]{1,0:T(8,128)(2,1)S(1)} %bitcast.24, f32[16,16,640]{2,1,0:T(8,128)S(1)} %bitcast.27), custom_call_target="tpu_custom_call" | custom-call | tf_op jit(solution)/shard_map/update/pallas_call | solution.py:247
  142.3 2.8 %update.3 = (f32[16,40]{1,0:T(8,128)}, bf16[32,20480]{1,0:T(8,128)(2,1)}) custom-call(s32[3]{0:T(128)S(1)} %pad_add_fusion.where_ref, f32[32,16]{1,0:T(8,128)S(1)} %get-tuple-element.9.turned_ref, bf16[32,20480]{1,0:T(8,128)(2,1)S(1)} %bitcast.20, bf16[32,20480]{1,0:T(8,128)(2,1)S(1)} %bitcast.25, ...), custom_call_target="tpu_custom_call", output_to_operand_aliasing={{1}: (6, {})} | custom-call | tf_op jit(solution)/shard_map/update/pallas_call | solution.py:250
  (11 shorter events, 0.1 us)
Async XLA Ops:
  0.6 0.7 copy-start.4
  28.5 24.5 %copy-start.1 = (bf16[1,32,20480]{2,1,0:T(8,128)(2,1)S(1)}, bf16[1,32,20480]{2,1,0:T(8,128)(2,1)}, u32[]{:S(2)}) copy-start(bf16[1,32,20480]{2,1,0:T(8,128)(2,1)} %param.6) | copy-start | bytes 3932164
  28.7 24.3 %copy-start = (bf16[1,32,20480]{2,1,0:T(8,128)(2,1)S(1)}, bf16[1,32,20480]{2,1,0:T(8,128)(2,1)}, u32[]{:S(2)}) copy-start(bf16[1,32,20480]{2,1,0:T(8,128)(2,1)} %param.5) | copy-start | bytes 3932164
  28.7 24.3 %copy-start.3 = (s32[1,32,16]{1,2,0:T(8,128)S(1)}, s32[1,32,16]{1,2,0:T(8,128)}, u32[]{:S(2)}) copy-start(s32[1,32,16]{1,2,0:T(8,128)} %param.8) | copy-start | bytes 6148
  46.1 6.9 %collective-permute-start = (f32[16,80,128]{2,1,0:T(8,128)S(1)}, f32[16,80,128]{2,1,0:T(8,128)}, u32[]{:S(2)}, u32[]{:S(2)}) collective-permute-start(f32[16,80,128]{2,1,0:T(8,128)S(1)} %all_to_all.36.own_ref), channel_id=1, source_target_pairs={{0,1},{1,0},{2,3},{3,2},{4,5},{5,4},{6,7},{7,6},{8,9},{9,8},{10,11... | collective-permute-start | bytes 1966088 | tf_op jit(solution)/shard_map/gather_q_prev/ppermute | solution.py:209
  53.0 27.1 %copy-start.2 = (s32[1,20480,8]{1,2,0:T(8,128)S(1)}, s32[1,20480,8]{1,2,0:T(8,128)}, u32[]{:S(2)}) copy-start(s32[1,20480,8]{1,2,0:T(8,128)} %param.9) | copy-start | bytes 1966084
  82.2 5.3 %collective-permute-start.1 = (f32[16,16,640]{2,1,0:T(8,128)S(1)}, f32[16,16,640]{2,1,0:T(8,128)S(1)}, u32[]{:S(2)}, u32[]{:S(2)}) collective-permute-start(f32[16,16,640]{2,1,0:T(8,128)S(1)} %get-tuple-element.11), channel_id=1, source_target_pairs={{0,1},{1,0},{2,3},{3,2},{4,5},{5,4},{6,7},{7,6},{8,9},{9,8},{10,11... | collective-permute-start | bytes 1966088 | tf_op jit(solution)/shard_map/right_factor/ppermute | solution.py:229
  133.5 8.8 %collective-permute-start.2 = (f32[16,16,640]{2,1,0:T(8,128)S(1)}, f32[16,16,640]{2,1,0:T(8,128)}, u32[]{:S(2)}, u32[]{:S(2)}) collective-permute-start(f32[16,16,640]{2,1,0:T(8,128)S(1)} %bitcast.26), channel_id=1, source_target_pairs={{0,1},{1,0},{2,3},{3,2},{4,5},{5,4},{6,7},{7,6},{8,9},{9,8},{10,11... | collective-permute-start | bytes 1966088 | tf_op jit(solution)/shard_map/right_factor/ppermute | solution.py:242

commit v4 on v3

--- a/solution.py
+++ b/solution.py
@@ -55,8 +55,8 @@
         o_ref[s] = packed
 
 
-def left_factor(c_ref, grad_ref, res_ref, own_ref, other_ref, bits_ref, o_ref):
-    c = c_ref[0]
+def left_factor(grad_ref, res_ref, own_ref, other_ref, bits_ref, o_ref):
+    c = lax.axis_index("c")
     lane = lax.broadcasted_iota(jnp.int32, (ROWS, 128), 1)
     owner = lane % 8
     total = jnp.zeros((ROWS, 128), F32)
@@ -128,19 +128,19 @@
             o_ref[i * (STEP // BLOCK) + t] = sent[:, t * BLOCK : t * BLOCK + BLOCK]
 
 
-def right_first(c_ref, tiles_ref, grad_ref, res_ref, words_ref, basis_ref, o_ref):
+def right_first(tiles_ref, grad_ref, res_ref, words_ref, basis_ref, o_ref):
     total = tiles_ref[0]
     for s in range(1, tiles_ref.shape[0]):
         total = total + tiles_ref[s]
     rows = jnp.concatenate([total[:, r : r + 32] for r in range(0, 128, 32)], axis=0)
     basis = orthonormal(rows)
     basis_ref[...] = basis
-    half_columns(1 - c_ref[0], basis, grad_ref, res_ref, words_ref, o_ref)
-
-
-def right_second(c_ref, basis_ref, grad_ref, res_ref, words_ref, turned_ref, o_ref):
+    half_columns(1 - lax.axis_index("c"), basis, grad_ref, res_ref, words_ref, o_ref)
+
+
+def right_second(basis_ref, grad_ref, res_ref, words_ref, turned_ref, o_ref):
     turned_ref[...] = basis_ref[...].T
-    half_columns(c_ref[0], basis_ref[...], grad_ref, res_ref, words_ref, o_ref)
+    half_columns(lax.axis_index("c"), basis_ref[...], grad_ref, res_ref, words_ref, o_ref)
 
 
 def new_columns(side, turned_ref, grad_ref, res_ref, total_ref, o_ref, made_ref, sems):
@@ -162,15 +162,17 @@
     return copies
 
 
-def update_first(where_ref, turned_ref, grad_ref, res_ref, own_ref, o_ref, made_ref, sems):
-    for copy in new_columns(where_ref[0], turned_ref, grad_ref, res_ref, own_ref, o_ref, made_ref, sems):
+def update_first(turned_ref, grad_ref, res_ref, own_ref, o_ref, made_ref, sems):
+    for copy in new_columns(lax.axis_index("c"), turned_ref, grad_ref, res_ref, own_ref, o_ref, made_ref, sems):
         copy.wait()
 
 
 def update_second(
-    where_ref, turned_ref, grad_ref, res_ref, own_ref, rest_ref, done_ref, q_ref, o_ref, made_ref, sems
+    turned_ref, grad_ref, res_ref, own_ref, rest_ref, done_ref, q_ref, o_ref, made_ref, sems
 ):
-    c, block, offset = where_ref[0], where_ref[1], where_ref[2]
+    c = lax.axis_index("c")
+    device = ((lax.axis_index("zh") * 2 + lax.axis_index("zl")) * 16 + lax.axis_index("s")) * 2 + c
+    block, offset = device // 16, (device % 16) * 40
     copies = new_columns(1 - c, turned_ref, grad_ref, res_ref, rest_ref, o_ref, made_ref, sems)
     t = block % 16
     mine = jnp.where(block // 16 == c, own_ref[t], rest_ref[t])
@@ -188,12 +190,9 @@
     z, plane, group = ("zh", "zl"), ("s", "c"), ("zl", "s")
     grad, res = gradient[0], residual[0]
     p_words, q_words = p_bits[0].T, q_bits[0].T
-    c = lax.axis_index("c")
-    device = lax.axis_index(("zh", "zl", "s", "c"))
     swap = [(0, 1), (1, 0)]
     whole = pl.BlockSpec(memory_space=pltpu.VMEM)
     far = pl.BlockSpec(memory_space=pl.ANY)
-    scalars = pl.BlockSpec(memory_space=pltpu.SMEM)
 
     with jax.named_scope("gather_q_prev"):
         pieces = call(pack_factor, jax.ShapeDtypeStruct((16, 1, 640), F32), in_specs=[whole], out_specs=whole)(q_prev.T)
@@ -211,9 +210,9 @@
         tile = call(
             left_factor,
             jax.ShapeDtypeStruct((32, 4, 128), F32),
-            in_specs=[scalars] + [whole] * 5,
+            in_specs=[whole] * 5,
             out_specs=whole,
-        )(c.reshape(1), grad, res, own, other, p_words)
+        )(grad, res, own, other, p_words)
         tile = exchange(tile, plane)
         tile = call(add_and_repeat, jax.ShapeDtypeStruct((16, 4, 128), F32), in_specs=[whole], out_specs=whole)(tile)
         tile = exchange(tile, z)
@@ -223,16 +222,16 @@
         basis, away = call(
             right_first,
             (jax.ShapeDtypeStruct((16, 32), F32), half),
-            in_specs=[scalars] + [whole] * 4,
+            in_specs=[whole] * 4,
             out_specs=(whole, whole),
-        )(c.reshape(1), tile, grad, res, q_words)
+        )(tile, grad, res, q_words)
         away = lax.ppermute(away, "c", swap)
         turned, kept = call(
             right_second,
             (jax.ShapeDtypeStruct((32, 16), F32), half),
-            in_specs=[scalars] + [whole] * 4,
+            in_specs=[whole] * 4,
             out_specs=(whole, whole),
-        )(c.reshape(1), basis, grad, res, q_words)
+        )(basis, grad, res, q_words)
         summed = (kept + away).reshape(32, 8, BLOCK)
         summed = exchange(summed, group)
         summed = call(add_and_repeat, jax.ShapeDtypeStruct((8, 8, BLOCK), F32), in_specs=[whole], out_specs=whole)(summed)
@@ -241,20 +240,19 @@
         total = exchange(summed, group).reshape(16, 16, BLOCK)
         rest = lax.ppermute(total, "c", swap)
     with jax.named_scope("update"):
-        where = jnp.stack([c, device // 16, (device % 16) * 40])
         done = jax.ShapeDtypeStruct((ROWS, FF), BF16)
         room = [pltpu.VMEM((ROWS, HALF), BF16), pltpu.SemaphoreType.DMA((steps,))]
         updated = call(
-            update_first, done, in_specs=[scalars] + [whole] * 4, out_specs=far, scratch_shapes=room
-        )(where, turned, grad, res, total)
+            update_first, done, in_specs=[whole] * 4, out_specs=far, scratch_shapes=room
+        )(turned, grad, res, total)
         q_next, updated = call(
             update_second,
             (jax.ShapeDtypeStruct((16, 40), F32), done),
-            in_specs=[scalars] + [whole] * 5 + [far],
+            in_specs=[whole] * 5 + [far],
             out_specs=(whole, far),
             scratch_shapes=room,
-            input_output_aliases={6: 1},
-        )(where, turned, grad, res, total, rest, updated)
+            input_output_aliases={5: 1},
+        )(turned, grad, res, total, rest, updated)
     return (q_next.T, updated[None])
 
 

time: 146 us -> 143 us (0.979)
  Pallas kernels: 9.82 us -> 7.04 us
    pallas_call x2, Pallas kernels: 3.92 us -> 2.24 us  [the longest x1 1.14 us: shards(): call(update_first, done, in_specs=[whole] * 4, out_specs=far, scratch_sha...]
  transfers between devices with their start and end apart: 3 -> 3, of which waited for: 2 -> 3; matrix products, arithmetic and copies ran while one was open for 0% -> 0% of each run, Pallas kernels for 2% -> 1%
where the time goes in v4:
time: 143 us
  blocking collectives  115 us (80%)
  starting transfers between devices  15.6 us (11%)
  Pallas kernels  7.04 us (5%)
  waiting for transfers between devices  3.39 us (2%)
    all_to_all x7, blocking collectives, exchange(): return lax.all_to_all(blocks, axis, 0, 0, tiled=True)  115 us
    ppermute x1, starting transfers between devices, shards(): rest = lax.ppermute(total, 'c', swap)  6.98 us
    ppermute x1, starting transfers between devices, shards(): other = lax.ppermute(own, 'c', swap)  5.07 us
    ppermute x1, starting transfers between devices, shards(): away = lax.ppermute(away, 'c', swap)  3.57 us
  transfers between devices with their start and end apart: 3, of which 3 were waited for; matrix products, arithmetic and copies ran while one was open for 0% of the time, Pallas kernels for 1%

profile of v4, /device:TPU:1, one launch (start us, length us, event | category | flops | bytes accessed | tf_op | source)
XLA Modules:
  0.0 142.6 jit_solution(14067336002252969793)
XLA Ops:
  0.6 0.7 copy-done.4
  1.3 0.1 gather_q_prev.2
  1.4 27.1 %all_to_all.35.x_ref = f32[16,1,640]{2,1,0:T(1,128)S(1)} all-to-all(f32[16,1,640]{2,1,0:T(1,128)S(1)} %gather_q_prev.2), channel_id=1, replica_groups=mesh['zh'=8,'zl'=2,'s'=16,'c'=2] {'zh','zl'}, dimensions={0} | all-to-all | bytes 81920 | tf_op jit(solution)/shard_map/gather_q_prev/all_to_all | solution.py:186
  28.5 0.2 gather_q_prev.3
  28.7 17.4 %all_to_all.36.own_ref = f32[16,80,128]{2,1,0:T(8,128)S(1)} all-to-all(f32[16,80,128]{2,1,0:T(8,128)S(1)} %gather_q_prev.3), channel_id=1, replica_groups=mesh['zh'=8,'zl'=2,'s'=16,'c'=2] {'s'}, dimensions={0} | all-to-all | bytes 1310720 | tf_op jit(solution)/shard_map/gather_q_prev/all_to_all | solution.py:186
  46.1 5.1 %collective-permute-start = (f32[16,80,128]{2,1,0:T(8,128)S(1)}, f32[16,80,128]{2,1,0:T(8,128)S(1)}, u32[]{:S(2)}, u32[]{:S(2)}) collective-permute-start(f32[16,80,128]{2,1,0:T(8,128)S(1)} %all_to_all.36.own_ref), channel_id=1, source_target_pairs={{0,1},{1,0},{2,3},{3,2},{4,5},{5,4},{6,7},{7,6},{8,9},{9,8},{10,11... | collective-permute-start | bytes 1966088 | tf_op jit(solution)/shard_map/gather_q_prev/ppermute | solution.py:208
  51.2 1.7 %collective-permute-done.other_ref = f32[16,80,128]{2,1,0:T(8,128)S(1)} collective-permute-done((f32[16,80,128]{2,1,0:T(8,128)S(1)}, f32[16,80,128]{2,1,0:T(8,128)S(1)}, u32[]{:S(2)}, u32[]{:S(2)}) %collective-permute-start) | collective-permute-done | bytes 655392 | tf_op jit(solution)/shard_map/gather_q_prev/ppermute | solution.py:208
  52.9 1.1 left_factor.2
  54.0 10.8 %all_to_all.37.x_ref = f32[32,4,128]{2,1,0:T(4,128)S(1)} all-to-all(f32[32,4,128]{2,1,0:T(4,128)S(1)} %left_factor.2), channel_id=1, replica_groups=mesh['zh'=8,'zl'=2,'s'=16,'c'=2] {'s','c'}, dimensions={0} | all-to-all | bytes 131072 | tf_op jit(solution)/shard_map/left_factor/all_to_all | solution.py:186
  64.9 14.0 %all_to_all.38.tiles_ref = f32[16,4,128]{2,1,0:T(4,128)S(1)} all-to-all(f32[16,4,128]{2,1,0:T(4,128)S(1)} %left_factor.3), channel_id=1, replica_groups=mesh['zh'=8,'zl'=2,'s'=16,'c'=2] {'zh','zl'}, dimensions={0} | all-to-all | bytes 65536 | tf_op jit(solution)/shard_map/left_factor/all_to_all | solution.py:186
  78.8 2.1 %right_factor.4 = (f32[16,32]{1,0:T(8,128)S(1)}, f32[16,16,640]{2,1,0:T(8,128)S(1)}) custom-call(f32[16,4,128]{2,1,0:T(4,128)S(1)} %all_to_all.38.tiles_ref, bf16[32,20480]{1,0:T(8,128)(2,1)S(1)} %bitcast.14, bf16[32,20480]{1,0:T(8,128)(2,1)S(1)} %bitcast.19, s32[8,20480]{1,0:T(8,128)S(1)} %bitcast.26), custom_call_target="tpu_custom_call" | custom-call | tf_op jit(solution)/shard_map/right_factor/pallas_call | solution.py:222
  80.9 3.6 %collective-permute-start.1 = (f32[16,16,640]{2,1,0:T(8,128)S(1)}, f32[16,16,640]{2,1,0:T(8,128)S(1)}, u32[]{:S(2)}, u32[]{:S(2)}) collective-permute-start(f32[16,16,640]{2,1,0:T(8,128)S(1)} %get-tuple-element.11), channel_id=1, source_target_pairs={{0,1},{1,0},{2,3},{3,2},{4,5},{5,4},{6,7},{7,6},{8,9},{9,8},{10,11... | collective-permute-start | bytes 1966088 | tf_op jit(solution)/shard_map/right_factor/ppermute | solution.py:228
  84.5 0.6 right_factor.5
  85.1 1.1 collective-permute-done.1
  86.2 0.1 add.3
  86.3 14.4 %all_to_all.39.x_ref = f32[32,8,640]{2,1,0:T(8,128)S(1)} all-to-all(f32[32,8,640]{2,1,0:T(8,128)S(1)} %bitcast.31), channel_id=1, replica_groups=mesh['zh'=8,'zl'=2,'s'=16,'c'=2] {'zl','s'}, dimensions={0} | all-to-all | bytes 1310720 | tf_op jit(solution)/shard_map/right_factor/all_to_all | solution.py:186
  100.7 0.1 right_factor.6
  100.8 17.1 %all_to_all.40.x_ref = f32[8,8,640]{2,1,0:T(8,128)S(1)} all-to-all(f32[8,8,640]{2,1,0:T(8,128)S(1)} %right_factor.6), channel_id=1, replica_groups=mesh['zh'=8,'zl'=2,'s'=16,'c'=2] {'zh'}, dimensions={0} | all-to-all | bytes 327680 | tf_op jit(solution)/shard_map/right_factor/all_to_all | solution.py:186
  117.9 0.1 right_factor.7
  117.9 14.3 %all_to_all.41 = f32[32,8,640]{2,1,0:T(8,128)S(1)} all-to-all(f32[32,8,640]{2,1,0:T(8,128)S(1)} %right_factor.7), channel_id=1, replica_groups=mesh['zh'=8,'zl'=2,'s'=16,'c'=2] {'zl','s'}, dimensions={0} | all-to-all | bytes 1310720 | tf_op jit(solution)/shard_map/right_factor/all_to_all | solution.py:186
  132.2 7.0 %collective-permute-start.2 = (f32[16,16,640]{2,1,0:T(8,128)S(1)}, f32[16,16,640]{2,1,0:T(8,128)S(1)}, u32[]{:S(2)}, u32[]{:S(2)}) collective-permute-start(f32[16,16,640]{2,1,0:T(8,128)S(1)} %bitcast.23), channel_id=1, source_target_pairs={{0,1},{1,0},{2,3},{3,2},{4,5},{5,4},{6,7},{7,6},{8,9},{9,8},{10,11... | collective-permute-start | bytes 1966088 | tf_op jit(solution)/shard_map/right_factor/ppermute | solution.py:241
  139.2 1.1 update.2.done_ref
  140.4 0.6 collective-permute-done.2.rest_ref
  140.9 1.7 %update.3 = (f32[16,40]{1,0:T(8,128)}, bf16[32,20480]{1,0:T(8,128)(2,1)}) custom-call(f32[32,16]{1,0:T(8,128)S(1)} %get-tuple-element.9.turned_ref, bf16[32,20480]{1,0:T(8,128)(2,1)S(1)} %bitcast.17, bf16[32,20480]{1,0:T(8,128)(2,1)S(1)} %bitcast.22, f32[16,16,640]{2,1,0:T(8,128)S(1)} %bitcast.25, ...), custom_call_target="tpu_custom_call", output_to_operand_aliasing={{1}: (5, {})} | custom-call | tf_op jit(solution)/shard_map/update/pallas_call | solution.py:248
  (10 shorter events, 0.1 us)
Async XLA Ops:
  0.6 0.7 copy-start.4
  28.5 24.4 %copy-start.1 = (bf16[1,32,20480]{2,1,0:T(8,128)(2,1)S(1)}, bf16[1,32,20480]{2,1,0:T(8,128)(2,1)}, u32[]{:S(2)}) copy-start(bf16[1,32,20480]{2,1,0:T(8,128)(2,1)} %param.6) | copy-start | bytes 3932164
  28.5 24.4 %copy-start.3 = (s32[1,32,16]{1,2,0:T(8,128)S(1)}, s32[1,32,16]{1,2,0:T(8,128)}, u32[]{:S(2)}) copy-start(s32[1,32,16]{1,2,0:T(8,128)} %param.8) | copy-start | bytes 6148
  28.7 24.2 %copy-start = (bf16[1,32,20480]{2,1,0:T(8,128)(2,1)S(1)}, bf16[1,32,20480]{2,1,0:T(8,128)(2,1)}, u32[]{:S(2)}) copy-start(bf16[1,32,20480]{2,1,0:T(8,128)(2,1)} %param.5) | copy-start | bytes 3932164
  46.1 6.8 %collective-permute-start = (f32[16,80,128]{2,1,0:T(8,128)S(1)}, f32[16,80,128]{2,1,0:T(8,128)S(1)}, u32[]{:S(2)}, u32[]{:S(2)}) collective-permute-start(f32[16,80,128]{2,1,0:T(8,128)S(1)} %all_to_all.36.own_ref), channel_id=1, source_target_pairs={{0,1},{1,0},{2,3},{3,2},{4,5},{5,4},{6,7},{7,6},{8,9},{9,8},{10,11... | collective-permute-start | bytes 1966088 | tf_op jit(solution)/shard_map/gather_q_prev/ppermute | solution.py:208
  52.9 25.9 %copy-start.2 = (s32[1,20480,8]{1,2,0:T(8,128)S(1)}, s32[1,20480,8]{1,2,0:T(8,128)}, u32[]{:S(2)}) copy-start(s32[1,20480,8]{1,2,0:T(8,128)} %param.9) | copy-start | bytes 1966084
  80.9 5.3 %collective-permute-start.1 = (f32[16,16,640]{2,1,0:T(8,128)S(1)}, f32[16,16,640]{2,1,0:T(8,128)S(1)}, u32[]{:S(2)}, u32[]{:S(2)}) collective-permute-start(f32[16,16,640]{2,1,0:T(8,128)S(1)} %get-tuple-element.11), channel_id=1, source_target_pairs={{0,1},{1,0},{2,3},{3,2},{4,5},{5,4},{6,7},{7,6},{8,9},{9,8},{10,11... | collective-permute-start | bytes 1966088 | tf_op jit(solution)/shard_map/right_factor/ppermute | solution.py:228
  132.2 8.7 %collective-permute-start.2 = (f32[16,16,640]{2,1,0:T(8,128)S(1)}, f32[16,16,640]{2,1,0:T(8,128)S(1)}, u32[]{:S(2)}, u32[]{:S(2)}) collective-permute-start(f32[16,16,640]{2,1,0:T(8,128)S(1)} %bitcast.23), channel_id=1, source_target_pairs={{0,1},{1,0},{2,3},{3,2},{4,5},{5,4},{6,7},{7,6},{8,9},{9,8},{10,11... | collective-permute-start | bytes 1966088 | tf_op jit(solution)/shard_map/right_factor/ppermute | solution.py:241

commit v5 on v4

--- a/solution.py
+++ b/solution.py
@@ -14,17 +14,18 @@
 HALF = FF // 2
 BLOCK = 640
 STEP = 2560
+SHARE = 2560
 WIDTH = 0.25
 F32 = jnp.float32
 BF16 = jnp.bfloat16
 VMEM_LIMIT = 16 * 1024 * 1024
 
 
-def call(body, out_shape, **kw):
+def call(body, out_shape, limit=VMEM_LIMIT, **kw):
     return pl.pallas_call(
         body,
         out_shape=out_shape,
-        compiler_params=pltpu.CompilerParams(vmem_limit_bytes=VMEM_LIMIT),
+        compiler_params=pltpu.CompilerParams(vmem_limit_bytes=limit),
         **kw,
     )
 
@@ -44,48 +45,86 @@
         o_ref[z] = flat
 
 
+def share(far_grad_ref, far_res_ref, far_words_ref, bits_ref, far_ref, grad_ref, res_ref, words_ref, o_ref, sems):
+    pairs = ((far_grad_ref, grad_ref), (far_res_ref, res_ref), (far_words_ref, words_ref))
+    copies = []
+    for i in range(FF // SHARE):
+        at = pl.ds(i * SHARE, SHARE)
+        copies.append([pltpu.make_async_copy(far.at[:, at], near.at[:, at], sems.at[i, k]) for k, (far, near) in enumerate(pairs)])
+        for copy in copies[i]:
+            copy.start()
+    bits = bits_ref[...].astype(F32)
+    o_ref[0:8, FF:] = jnp.concatenate([bits[0:8], bits[8:16], jnp.zeros((8, 64), F32)], axis=1)
+    for i in range(FF // SHARE):
+        at = pl.ds(i * SHARE, SHARE)
+        for copy in copies[i]:
+            copy.wait()
+        o_ref[0:ROWS, at] = grad_ref[:, at].astype(F32) + res_ref[:, at].astype(F32)
+        o_ref[ROWS : ROWS + 8, at] = words_ref[:, at].astype(F32)
+        last = FF + 128 if i == FF // SHARE - 1 else i * SHARE + SHARE
+        here = pl.ds(i * SHARE, last - i * SHARE)
+        copies.append(pltpu.make_async_copy(o_ref.at[:, here], far_ref.at[:, here], sems.at[i, 3]))
+        copies[-1].start()
+    for copy in copies[FF // SHARE :]:
+        copy.wait()
+
+
 def spread_factor(x_ref, o_ref):
     pieces = x_ref[:, 0, :]
-    halves = []
-    for g in range(2):
-        rows = [pieces[g * 8 : g * 8 + 8, r * 40 : r * 40 + 40] for r in range(RANK)]
-        halves.append(jnp.concatenate(rows, axis=0).T)
-    packed = jnp.concatenate(halves, axis=0)
-    for s in range(o_ref.shape[0]):
-        o_ref[s] = packed
-
-
-def left_factor(grad_ref, res_ref, own_ref, other_ref, bits_ref, o_ref):
+    for half in range(2):
+        rows = [pieces[:, r * 40 : r * 40 + 40] for r in range(half * 8, half * 8 + 8)]
+        packed = jnp.concatenate(rows, axis=0).T
+        for s in range(16):
+            o_ref[s * 2 + half] = packed
+
+
+def left_factor(grad_ref, res_ref, other_ref, factor_ref, bits_ref, o_ref):
     c = lax.axis_index("c")
-    lane = lax.broadcasted_iota(jnp.int32, (ROWS, 128), 1)
-    owner = lane % 8
-    total = jnp.zeros((ROWS, 128), F32)
-    for g in range(2):
-        chunks = []
-        for s in range(16):
-            a = own_ref[s, g * 40 : g * 40 + 40, :]
-            b = other_ref[s, g * 40 : g * 40 + 40, :]
-            chunks.append(jnp.where(c == 0, a, b))
-            chunks.append(jnp.where(c == 0, b, a))
-        factor = jnp.concatenate(chunks, axis=0)
-        factor = jnp.concatenate(parts(factor, 2), axis=1)
-        rows = [ref[:, z * 1280 : z * 1280 + 1280] for ref in (grad_ref, res_ref) for z in range(g * 8, g * 8 + 8)]
+    factor = jnp.concatenate(parts(factor_ref[...].reshape(1280, 128), 2), axis=1)
+    owner = lax.broadcasted_iota(jnp.int32, (ROWS, 128), 1) % 16
+    totals = [jnp.zeros((ROWS, 128), F32), jnp.zeros((ROWS, 128), F32)]
+    for z in range(0, 16, 4):
+        places = [slice(k * 1280, k * 1280 + 1280) for k in range(z, z + 4)]
+        split = [parts(other_ref[0:ROWS, at], 2) for at in places]
+        rows = [grad_ref[:, at] for at in places] + [res_ref[:, at] for at in places]
+        rows += [high for high, _ in split] + [low for _, low in split]
         prod = jnp.dot(jnp.concatenate(rows, axis=0), factor, preferred_element_type=F32)
-        prod = prod[0:256] + prod[256:512]
         prod = prod[:, 0:128] + prod[:, 128:256]
-        for e in range(8):
-            total = total + jnp.where(owner == e, prod[e * 32 : e * 32 + 32], 0.0)
-    rank = lax.broadcasted_iota(jnp.int32, (RANK, 128), 0)
-    lane = lax.broadcasted_iota(jnp.int32, (RANK, 128), 1)
-    fold = jnp.where(lane // 8 == rank, 1.0, 0.0).astype(F32)
-    local = lax.dot_general(
-        fold, total, (((1,), (1,)), ((), ())), precision=lax.Precision.HIGHEST, preferred_element_type=F32
+        for w in range(2):
+            both = prod[w * 256 : w * 256 + 128] + prod[w * 256 + 128 : w * 256 + 256]
+            for k in range(4):
+                totals[w] = totals[w] + jnp.where(owner == z + k, both[k * 32 : k * 32 + 32], 0.0)
+    rank = lax.broadcasted_iota(jnp.int32, (8, 128), 0)
+    lane = lax.broadcasted_iota(jnp.int32, (8, 128), 1)
+    fold = jnp.where(lane // 16 == rank, 1.0, 0.0).astype(F32)
+    here = bits_ref[...].astype(F32)
+    there = other_ref[0:8, FF:]
+    bits = (
+        jnp.where(c == 0, here[0:8], here[8:16]),
+        jnp.where(c == 0, there[:, 0:32], there[:, 32:64]),
     )
-    noise = bits_ref[...].astype(F32) * 2.0 ** (-21) - 0.5
-    sent = (local + noise * WIDTH * jnp.abs(local)).astype(BF16).astype(F32)
-    tile = jnp.concatenate([sent[r : r + 4] for r in range(0, RANK, 4)], axis=1)
+    sent = jnp.zeros((8, 32), F32)
+    for w in range(2):
+        local = lax.dot_general(
+            fold, totals[w], (((1,), (1,)), ((), ())), precision=lax.Precision.HIGHEST, preferred_element_type=F32
+        )
+        noise = bits[w] * 2.0 ** (-21) - 0.5
+        sent = sent + (local + noise * WIDTH * jnp.abs(local)).astype(BF16).astype(F32)
+    tile = jnp.concatenate([sent[r : r + 2] for r in range(0, 8, 2)], axis=1)
     for s in range(o_ref.shape[0]):
         o_ref[s] = tile
+
+
+def add_left(x_ref, o_ref):
+    halves = []
+    for c in range(2):
+        total = x_ref[c]
+        for s in range(1, 16):
+            total = total + x_ref[s * 2 + c]
+        halves.append(total)
+    both = jnp.concatenate(halves, axis=0)
+    for z in range(o_ref.shape[0]):
+        o_ref[z] = both
 
 
 def add_and_repeat(x_ref, o_ref):
@@ -108,11 +147,8 @@
     return rows
 
 
-def right_columns(basis, grad, res, words):
-    split = jnp.concatenate(parts(basis, 3), axis=0)
-    split = jnp.concatenate([split, split], axis=1)
-    both = jnp.concatenate([grad, res], axis=0)
-    prod = jnp.dot(split, both, preferred_element_type=F32)
+def right_columns(split, first, second, words):
+    prod = jnp.dot(split, jnp.concatenate([first, second], axis=0), preferred_element_type=F32)
     local = prod[0:16] + prod[16:32] + prod[32:48]
     low = (words & 127).astype(F32) * (1.0 / 128.0)
     high = (words >> 7).astype(F32) * (1.0 / 64.0)
@@ -120,27 +156,23 @@
     return (local + noise * WIDTH * jnp.abs(local)).astype(BF16).astype(F32)
 
 
-def half_columns(side, basis, grad_ref, res_ref, words_ref, o_ref):
-    for i in range(HALF // STEP):
-        at = pl.ds(pl.multiple_of(side * HALF + i * STEP, STEP), STEP)
-        sent = right_columns(basis, grad_ref[:, at], res_ref[:, at], words_ref[:, at])
-        for t in range(STEP // BLOCK):
-            o_ref[i * (STEP // BLOCK) + t] = sent[:, t * BLOCK : t * BLOCK + BLOCK]
-
-
-def right_first(tiles_ref, grad_ref, res_ref, words_ref, basis_ref, o_ref):
+def right_factor(tiles_ref, grad_ref, res_ref, words_ref, other_ref, turned_ref, o_ref):
     total = tiles_ref[0]
     for s in range(1, tiles_ref.shape[0]):
         total = total + tiles_ref[s]
-    rows = jnp.concatenate([total[:, r : r + 32] for r in range(0, 128, 32)], axis=0)
-    basis = orthonormal(rows)
-    basis_ref[...] = basis
-    half_columns(1 - lax.axis_index("c"), basis, grad_ref, res_ref, words_ref, o_ref)
-
-
-def right_second(basis_ref, grad_ref, res_ref, words_ref, turned_ref, o_ref):
-    turned_ref[...] = basis_ref[...].T
-    half_columns(lax.axis_index("c"), basis_ref[...], grad_ref, res_ref, words_ref, o_ref)
+    rows = [total[c * 2 : c * 2 + 2, q * 32 : q * 32 + 32] for c in range(2) for q in range(4)]
+    basis = orthonormal(jnp.concatenate(rows, axis=0))
+    turned_ref[...] = basis.T
+    split = jnp.concatenate(parts(basis, 3), axis=0)
+    split = jnp.concatenate([split, split], axis=1)
+    base = lax.axis_index("c") * HALF
+    for i in range(HALF // STEP):
+        at = pl.ds(pl.multiple_of(base + i * STEP, STEP), STEP)
+        sent = right_columns(split, grad_ref[:, at], res_ref[:, at], words_ref[:, at])
+        high, low = parts(other_ref[0:ROWS, at], 2)
+        sent = sent + right_columns(split, high, low, other_ref[ROWS : ROWS + 8, at].astype(jnp.int32))
+        for t in range(STEP // BLOCK):
+            o_ref[i * (STEP // BLOCK) + t] = sent[:, t * BLOCK : t * BLOCK + BLOCK]
 
 
 def new_columns(side, turned_ref, grad_ref, res_ref, total_ref, o_ref, made_ref, sems):
@@ -194,45 +226,49 @@
     whole = pl.BlockSpec(memory_space=pltpu.VMEM)
     far = pl.BlockSpec(memory_space=pl.ANY)
 
+    with jax.named_scope("share"):
+        mine = call(
+            share,
+            jax.ShapeDtypeStruct((ROWS + 8, FF + 128), F32),
+            limit=56 * 1024 * 1024,
+            in_specs=[far, far, far, whole],
+            out_specs=far,
+            scratch_shapes=[
+                pltpu.VMEM((ROWS, FF), BF16),
+                pltpu.VMEM((ROWS, FF), BF16),
+                pltpu.VMEM((8, FF), jnp.int32),
+                pltpu.VMEM((ROWS + 8, FF + 128), F32),
+                pltpu.SemaphoreType.DMA((FF // SHARE, 4)),
+            ],
+        )(grad, res, q_words, p_words)
+        other = lax.ppermute(mine, "c", swap)
     with jax.named_scope("gather_q_prev"):
         pieces = call(pack_factor, jax.ShapeDtypeStruct((16, 1, 640), F32), in_specs=[whole], out_specs=whole)(q_prev.T)
         pieces = exchange(pieces, z)
         spread = call(
             spread_factor,
-            jax.ShapeDtypeStruct((16, 80, 128), F32),
+            jax.ShapeDtypeStruct((32, 40, 128), F32),
             in_specs=[whole],
             out_specs=whole,
             cost_estimate=pl.CostEstimate(flops=10**11, bytes_accessed=10**8, transcendentals=0),
         )(pieces)
-        own = exchange(spread, "s")
-        other = lax.ppermute(own, "c", swap)
+        factor = exchange(spread, plane)
     with jax.named_scope("left_factor"):
-        tile = call(
-            left_factor,
-            jax.ShapeDtypeStruct((32, 4, 128), F32),
-            in_specs=[whole] * 5,
-            out_specs=whole,
-        )(grad, res, own, other, p_words)
+        tile = call(left_factor, jax.ShapeDtypeStruct((32, 2, 128), F32), in_specs=[whole] * 5, out_specs=whole)(
+            grad, res, other, factor, p_words
+        )
         tile = exchange(tile, plane)
-        tile = call(add_and_repeat, jax.ShapeDtypeStruct((16, 4, 128), F32), in_specs=[whole], out_specs=whole)(tile)
+        tile = call(add_left, jax.ShapeDtypeStruct((16, 4, 128), F32), in_specs=[whole], out_specs=whole)(tile)
         tile = exchange(tile, z)
     steps = HALF // STEP
     with jax.named_scope("right_factor"):
-        half = jax.ShapeDtypeStruct((16, 16, BLOCK), F32)
-        basis, away = call(
-            right_first,
-            (jax.ShapeDtypeStruct((16, 32), F32), half),
-            in_specs=[whole] * 4,
+        turned, summed = call(
+            right_factor,
+            (jax.ShapeDtypeStruct((32, 16), F32), jax.ShapeDtypeStruct((16, 16, BLOCK), F32)),
+            in_specs=[whole] * 5,
             out_specs=(whole, whole),
-        )(tile, grad, res, q_words)
-        away = lax.ppermute(away, "c", swap)
-        turned, kept = call(
-            right_second,
-            (jax.ShapeDtypeStruct((32, 16), F32), half),
-            in_specs=[whole] * 4,
-            out_specs=(whole, whole),
-        )(basis, grad, res, q_words)
-        summed = (kept + away).reshape(32, 8, BLOCK)
+        )(tile, grad, res, q_words, other)
+        summed = summed.reshape(32, 8, BLOCK)
         summed = exchange(summed, group)
         summed = call(add_and_repeat, jax.ShapeDtypeStruct((8, 8, BLOCK), F32), in_specs=[whole], out_specs=whole)(summed)
         summed = exchange(summed, "zh")

time: 143 us -> 139 us (0.972)
  blocking collectives: 115 us -> 93 us
  starting transfers between devices: 15.6 us -> 26.1 us
  Pallas kernels: 7.04 us -> 12 us
  waiting for transfers between devices: 3.39 us -> 5.39 us
    all_to_all x7 -> x6, blocking collectives: 115 us -> 93 us  [exchange(): return lax.all_to_all(blocks, axis, 0, 0, tiled=True)]
    all_to_all x0 -> x1, starting transfers between devices: none -> 15.7 us  [exchange(): return lax.all_to_all(blocks, axis, 0, 0, tiled=True)]
    ppermute x2 -> x1, starting transfers between devices: 8.64 us -> 2.86 us  [shards(): other = lax.ppermute(mine, 'c', swap)]
    all_to_all x0 -> x1, waiting for transfers between devices: none -> 4.85 us  [exchange(): return lax.all_to_all(blocks, axis, 0, 0, tiled=True)]
    pallas_call x5, Pallas kernels: 3.98 us -> 8.28 us  [the longest x1 3.79 us: shards(): call(share, jax.ShapeDtypeStruct((ROWS + 8, FF + 128), F32), limit=56 * 1...]
    ppermute x2 -> x1, waiting for transfers between devices: 2.84 us -> 0.01 us  [shards(): other = lax.ppermute(mine, 'c', swap)]
  transfers between devices with their start and end apart: 3 -> 3, of which waited for: 3 -> 2; matrix products, arithmetic and copies ran while one was open for 0% -> 0% of each run, Pallas kernels for 1% -> 4%
where the time goes in v5:
time: 139 us; the launch traced here: 138 us
  blocking collectives  93 us (67%)
  starting transfers between devices  26.1 us (19%)
  Pallas kernels  12 us (9%)
  waiting for transfers between devices  5.39 us (4%)
    all_to_all x6, blocking collectives, exchange(): return lax.all_to_all(blocks, axis, 0, 0, tiled=True)  93 us
    all_to_all x1, starting transfers between devices, exchange(): return lax.all_to_all(blocks, axis, 0, 0, tiled=True)  15.7 us
    ppermute x1, starting transfers between devices, shards(): rest = lax.ppermute(total, 'c', swap)  7.5 us
    all_to_all x1, waiting for transfers between devices, exchange(): return lax.all_to_all(blocks, axis, 0, 0, tiled=True)  4.85 us
    pallas_call x1, Pallas kernels, shards(): call(share, jax.ShapeDtypeStruct((ROWS + 8, FF + 128), F32), limit=56 * 1...  3.79 us
    ppermute x1, starting transfers between devices, shards(): other = lax.ppermute(mine, 'c', swap)  2.86 us
  transfers between devices with their start and end apart: 3, of which 2 were waited for; matrix products, arithmetic and copies ran while one was open for 0% of the time, Pallas kernels for 4%

profile of v5, /device:TPU:1, one launch (start us, length us, event | category | flops | bytes accessed | tf_op | source)
XLA Modules:
  0.0 138.0 jit_solution(14970981765766424812)
XLA Ops:
  0.6 0.0 copy-start.4
  0.6 0.7 copy-done.4
  1.3 0.7 gather_q_prev.2
  2.0 15.7 %all-to-all-start = ((f32[16,1,640]{2,1,0:T(1,128)}), f32[16,1,640]{2,1,0:T(1,128)S(1)}, u32[]{:S(2)}, u32[]{:S(2)}) async-start(f32[16,1,640]{2,1,0:T(1,128)} %gather_q_prev.2), calls=%async_computation | async-start | bytes 81920 | tf_op jit(solution)/shard_map/gather_q_prev/all_to_all | solution.py:218
  17.8 3.8 %share.1 = f32[40,20608]{1,0:T(8,128)} custom-call(bf16[32,20480]{1,0:T(8,128)(2,1)} %bitcast.13, bf16[32,20480]{1,0:T(8,128)(2,1)} %bitcast.18, s32[8,20480]{1,0:T(8,128)} %bitcast.26, s32[16,32]{1,0:T(8,128)} %bitcast.29), custom_call_target="tpu_custom_call" | custom-call | tf_op jit(solution)/shard_map/share/pallas_call | solution.py:230
  21.6 2.9 %collective-permute-start = (f32[40,20608]{1,0:T(8,128)}, f32[40,20608]{1,0:T(8,128)S(1)}, u32[]{:S(2)}, u32[]{:S(2)}) collective-permute-start(f32[40,20608]{1,0:T(8,128)} %share.1), channel_id=1, source_target_pairs={{0,1},{1,0},{2,3},{3,2},{4,5},{5,4},{6,7},{7,6},{8,9},{9,8},{10,11... | collective-permute-start | bytes 9891848 | tf_op jit(solution)/shard_map/share/ppermute | solution.py:244
  24.5 4.8 %all-to-all-done.x_ref = f32[16,1,640]{2,1,0:T(1,128)S(1)} async-done(((f32[16,1,640]{2,1,0:T(1,128)}), f32[16,1,640]{2,1,0:T(1,128)S(1)}, u32[]{:S(2)}, u32[]{:S(2)}) %all-to-all-start) | async-done | bytes 40992 | tf_op jit(solution)/shard_map/gather_q_prev/all_to_all | solution.py:218
  29.3 0.2 gather_q_prev.3
  29.5 0.0 copy-start
  29.5 22.0 %all_to_all.35.factor_ref = f32[32,40,128]{2,1,0:T(8,128)S(1)} all-to-all(f32[32,40,128]{2,1,0:T(8,128)S(1)} %gather_q_prev.3), channel_id=1, replica_groups=mesh['zh'=8,'zl'=2,'s'=16,'c'=2] {'s','c'}, dimensions={0} | all-to-all | bytes 1310720 | tf_op jit(solution)/shard_map/gather_q_prev/all_to_all | solution.py:218
  51.5 0.0 collective-permute-done.other_ref
  51.5 1.8 %left_factor.2 = f32[32,2,128]{2,1,0:T(2,128)S(1)} custom-call(bf16[32,20480]{1,0:T(8,128)(2,1)S(1)} %bitcast.14, bf16[32,20480]{1,0:T(8,128)(2,1)S(1)} %bitcast.19, f32[40,20608]{1,0:T(8,128)S(1)} %collective-permute-done.other_ref, f32[32,40,128]{2,1,0:T(8,128)S(1)} %all_to_all.35.factor_ref, s32[16,32]{1,0:T(8,128)S(1)} %bitcast.30), custom_call_target="tpu_custom_call" | custom-call | tf_op jit(solution)/shard_map/left_factor/pallas_call | solution.py:257
  53.3 10.8 %all_to_all.36.x_ref = f32[32,2,128]{2,1,0:T(2,128)S(1)} all-to-all(f32[32,2,128]{2,1,0:T(2,128)S(1)} %left_factor.2), channel_id=1, replica_groups=mesh['zh'=8,'zl'=2,'s'=16,'c'=2] {'s','c'}, dimensions={0} | all-to-all | bytes 65536 | tf_op jit(solution)/shard_map/left_factor/all_to_all | solution.py:218
  64.2 16.3 %all_to_all.37.tiles_ref = f32[16,4,128]{2,1,0:T(4,128)S(1)} all-to-all(f32[16,4,128]{2,1,0:T(4,128)S(1)} %left_factor.3), channel_id=1, replica_groups=mesh['zh'=8,'zl'=2,'s'=16,'c'=2] {'zh','zl'}, dimensions={0} | all-to-all | bytes 65536 | tf_op jit(solution)/shard_map/left_factor/all_to_all | solution.py:218
  80.5 2.5 %right_factor.3 = (f32[32,16]{1,0:T(8,128)S(1)}, f32[16,16,640]{2,1,0:T(8,128)S(1)}) custom-call(f32[16,4,128]{2,1,0:T(4,128)S(1)} %all_to_all.37.tiles_ref, bf16[32,20480]{1,0:T(8,128)(2,1)S(1)} %bitcast.15, bf16[32,20480]{1,0:T(8,128)(2,1)S(1)} %bitcast.20, s32[8,20480]{1,0:T(8,128)S(1)} %bitcast.27, f32[40,20608]{1,0:T(8,128)S(1)} %collective-permute-done.other_ref), custom_call_target="tpu_custom_call" | custom-call | tf_op jit(solution)/shard_map/right_factor/pallas_call | solution.py:265
  82.9 13.5 %all_to_all.38.x_ref = f32[32,8,640]{2,1,0:T(8,128)S(1)} all-to-all(f32[32,8,640]{2,1,0:T(8,128)S(1)} %bitcast.28), channel_id=1, replica_groups=mesh['zh'=8,'zl'=2,'s'=16,'c'=2] {'zl','s'}, dimensions={0} | all-to-all | bytes 1310720 | tf_op jit(solution)/shard_map/right_factor/all_to_all | solution.py:218
  96.4 0.1 right_factor.4
  96.4 17.2 %all_to_all.39.x_ref = f32[8,8,640]{2,1,0:T(8,128)S(1)} all-to-all(f32[8,8,640]{2,1,0:T(8,128)S(1)} %right_factor.4), channel_id=1, replica_groups=mesh['zh'=8,'zl'=2,'s'=16,'c'=2] {'zh'}, dimensions={0} | all-to-all | bytes 327680 | tf_op jit(solution)/shard_map/right_factor/all_to_all | solution.py:218
  113.6 0.1 right_factor.5
  113.7 13.3 %all_to_all.40 = f32[32,8,640]{2,1,0:T(8,128)S(1)} all-to-all(f32[32,8,640]{2,1,0:T(8,128)S(1)} %right_factor.5), channel_id=1, replica_groups=mesh['zh'=8,'zl'=2,'s'=16,'c'=2] {'zl','s'}, dimensions={0} | all-to-all | bytes 1310720 | tf_op jit(solution)/shard_map/right_factor/all_to_all | solution.py:218
  127.0 7.5 %collective-permute-start.1 = (f32[16,16,640]{2,1,0:T(8,128)S(1)}, f32[16,16,640]{2,1,0:T(8,128)S(1)}, u32[]{:S(2)}, u32[]{:S(2)}) collective-permute-start(f32[16,16,640]{2,1,0:T(8,128)S(1)} %bitcast.23), channel_id=1, source_target_pairs={{0,1},{1,0},{2,3},{3,2},{4,5},{5,4},{6,7},{7,6},{8,9},{9,8},{10,11... | collective-permute-start | bytes 1966088 | tf_op jit(solution)/shard_map/right_factor/ppermute | solution.py:277
  134.5 1.2 update.2.done_ref
  135.7 0.5 collective-permute-done.1.rest_ref
  136.2 1.7 %update.3 = (f32[16,40]{1,0:T(8,128)}, bf16[32,20480]{1,0:T(8,128)(2,1)}) custom-call(f32[32,16]{1,0:T(8,128)S(1)} %get-tuple-element.6.turned_ref, bf16[32,20480]{1,0:T(8,128)(2,1)S(1)} %bitcast.17, bf16[32,20480]{1,0:T(8,128)(2,1)S(1)} %bitcast.22, f32[16,16,640]{2,1,0:T(8,128)S(1)} %bitcast.25, ...), custom_call_target="tpu_custom_call", output_to_operand_aliasing={{1}: (5, {})} | custom-call | tf_op jit(solution)/shard_map/update/pallas_call | solution.py:284
  (8 shorter events, 0.0 us)
Async XLA Ops:
  0.6 0.7 copy-start.4
  2.0 27.3 %all-to-all-start = ((f32[16,1,640]{2,1,0:T(1,128)}), f32[16,1,640]{2,1,0:T(1,128)S(1)}, u32[]{:S(2)}, u32[]{:S(2)}) async-start(f32[16,1,640]{2,1,0:T(1,128)} %gather_q_prev.2), calls=%async_computation | async-start | bytes 81920 | tf_op jit(solution)/shard_map/gather_q_prev/all_to_all | solution.py:218
  21.6 29.9 %collective-permute-start = (f32[40,20608]{1,0:T(8,128)}, f32[40,20608]{1,0:T(8,128)S(1)}, u32[]{:S(2)}, u32[]{:S(2)}) collective-permute-start(f32[40,20608]{1,0:T(8,128)} %share.1), channel_id=1, source_target_pairs={{0,1},{1,0},{2,3},{3,2},{4,5},{5,4},{6,7},{7,6},{8,9},{9,8},{10,11... | collective-permute-start | bytes 9891848 | tf_op jit(solution)/shard_map/share/ppermute | solution.py:244
  29.3 22.2 %copy-start.1 = (bf16[1,32,20480]{2,1,0:T(8,128)(2,1)S(1)}, bf16[1,32,20480]{2,1,0:T(8,128)(2,1)}, u32[]{:S(2)}) copy-start(bf16[1,32,20480]{2,1,0:T(8,128)(2,1)} %param.6) | copy-start | bytes 3932164
  29.3 22.2 %copy-start.3 = (s32[1,32,16]{1,2,0:T(8,128)S(1)}, s32[1,32,16]{1,2,0:T(8,128)}, u32[]{:S(2)}) copy-start(s32[1,32,16]{1,2,0:T(8,128)} %param.8) | copy-start | bytes 6148
  29.5 22.0 %copy-start = (bf16[1,32,20480]{2,1,0:T(8,128)(2,1)S(1)}, bf16[1,32,20480]{2,1,0:T(8,128)(2,1)}, u32[]{:S(2)}) copy-start(bf16[1,32,20480]{2,1,0:T(8,128)(2,1)} %param.5) | copy-start | bytes 3932164
  51.5 29.0 %copy-start.2 = (s32[1,20480,8]{1,2,0:T(8,128)S(1)}, s32[1,20480,8]{1,2,0:T(8,128)}, u32[]{:S(2)}) copy-start(s32[1,20480,8]{1,2,0:T(8,128)} %param.9) | copy-start | bytes 1966084
  127.0 9.2 %collective-permute-start.1 = (f32[16,16,640]{2,1,0:T(8,128)S(1)}, f32[16,16,640]{2,1,0:T(8,128)S(1)}, u32[]{:S(2)}, u32[]{:S(2)}) collective-permute-start(f32[16,16,640]{2,1,0:T(8,128)S(1)} %bitcast.23), channel_id=1, source_target_pairs={{0,1},{1,0},{2,3},{3,2},{4,5},{5,4},{6,7},{7,6},{8,9},{9,8},{10,11... | collective-permute-start | bytes 1966088 | tf_op jit(solution)/shard_map/right_factor/ppermute | solution.py:277

commit v6 on v5

--- a/solution.py
+++ b/solution.py
@@ -14,7 +14,7 @@
 HALF = FF // 2
 BLOCK = 640
 STEP = 2560
-SHARE = 2560
+SHARE = 5120
 WIDTH = 0.25
 F32 = jnp.float32
 BF16 = jnp.bfloat16
@@ -45,28 +45,52 @@
         o_ref[z] = flat
 
 
-def share(far_grad_ref, far_res_ref, far_words_ref, bits_ref, far_ref, grad_ref, res_ref, words_ref, o_ref, sems):
-    pairs = ((far_grad_ref, grad_ref), (far_res_ref, res_ref), (far_words_ref, words_ref))
+def share(
+    far_grad_ref, far_res_ref, far_words_ref, far_bits_ref, far_ref, grad_ref, res_ref, words_ref, bits_ref, o_ref, sems
+):
+    theirs = pl.multiple_of((1 - lax.axis_index("c")) * HALF, HALF)
+    words = pltpu.make_async_copy(far_words_ref.at[:, pl.ds(theirs, HALF)], words_ref, sems.at[0, 2])
     copies = []
     for i in range(FF // SHARE):
         at = pl.ds(i * SHARE, SHARE)
-        copies.append([pltpu.make_async_copy(far.at[:, at], near.at[:, at], sems.at[i, k]) for k, (far, near) in enumerate(pairs)])
+        copies.append(
+            [
+                pltpu.make_async_copy(far_grad_ref.at[:, at], grad_ref.at[:, at], sems.at[i, 0]),
+                pltpu.make_async_copy(far_res_ref.at[:, at], res_ref.at[:, at], sems.at[i, 1]),
+            ]
+        )
         for copy in copies[i]:
             copy.start()
-    bits = bits_ref[...].astype(F32)
-    o_ref[0:8, FF:] = jnp.concatenate([bits[0:8], bits[8:16], jnp.zeros((8, 64), F32)], axis=1)
+    words.start()
+    late_bits = pltpu.make_async_copy(far_bits_ref, bits_ref, sems.at[2, 2])
+    late_bits.start()
+    sent = []
+
+    def send(start, size, sem):
+        at = pl.ds(start, size)
+        sent.append(pltpu.make_async_copy(o_ref.at[:, at], far_ref.at[:, at], sem))
+        sent[-1].start()
+
     for i in range(FF // SHARE):
         at = pl.ds(i * SHARE, SHARE)
         for copy in copies[i]:
             copy.wait()
-        o_ref[0:ROWS, at] = grad_ref[:, at].astype(F32) + res_ref[:, at].astype(F32)
-        o_ref[ROWS : ROWS + 8, at] = words_ref[:, at].astype(F32)
-        last = FF + 128 if i == FF // SHARE - 1 else i * SHARE + SHARE
-        here = pl.ds(i * SHARE, last - i * SHARE)
-        copies.append(pltpu.make_async_copy(o_ref.at[:, here], far_ref.at[:, here], sems.at[i, 3]))
-        copies[-1].start()
-    for copy in copies[FF // SHARE :]:
+        merged = grad_ref[:, at].astype(F32) + res_ref[:, at].astype(F32)
+        for k in range(4):
+            o_ref[:, k * FF + i * SHARE : k * FF + i * SHARE + SHARE] = merged[k * 8 : k * 8 + 8]
+            send(k * FF + i * SHARE, SHARE, sems.at[i, 3 + k])
+    words.wait()
+    late_bits.wait()
+    bits = bits_ref[...].astype(F32)
+    o_ref[:, 4 * FF + HALF :] = jnp.concatenate([bits[0:8], bits[8:16], jnp.zeros((8, 64), F32)], axis=1)
+    o_ref[:, 4 * FF : 4 * FF + HALF] = words_ref[...].astype(F32)
+    send(4 * FF, HALF + 128, sems.at[1, 2])
+    for copy in sent:
         copy.wait()
+
+
+def merged_of(other_ref, start, size):
+    return jnp.concatenate([other_ref[:, pl.ds(k * FF + start, size)] for k in range(4)], axis=0)
 
 
 def spread_factor(x_ref, o_ref):
@@ -85,7 +109,7 @@
     totals = [jnp.zeros((ROWS, 128), F32), jnp.zeros((ROWS, 128), F32)]
     for z in range(0, 16, 4):
         places = [slice(k * 1280, k * 1280 + 1280) for k in range(z, z + 4)]
-        split = [parts(other_ref[0:ROWS, at], 2) for at in places]
+        split = [parts(merged_of(other_ref, k * 1280, 1280), 2) for k in range(z, z + 4)]
         rows = [grad_ref[:, at] for at in places] + [res_ref[:, at] for at in places]
         rows += [high for high, _ in split] + [low for _, low in split]
         prod = jnp.dot(jnp.concatenate(rows, axis=0), factor, preferred_element_type=F32)
@@ -98,7 +122,7 @@
     lane = lax.broadcasted_iota(jnp.int32, (8, 128), 1)
     fold = jnp.where(lane // 16 == rank, 1.0, 0.0).astype(F32)
     here = bits_ref[...].astype(F32)
-    there = other_ref[0:8, FF:]
+    there = other_ref[:, 4 * FF + HALF :]
     bits = (
         jnp.where(c == 0, here[0:8], here[8:16]),
         jnp.where(c == 0, there[:, 0:32], there[:, 32:64]),
@@ -135,16 +159,16 @@
         o_ref[s] = total
 
 
-def orthonormal(rows):
-    index = lax.broadcasted_iota(jnp.int32, (RANK, 1), 0)
+def orthonormal(columns):
+    left = [jnp.broadcast_to(columns[:, k : k + 1], (ROWS, 128)) for k in range(RANK)]
+    lane = lax.broadcasted_iota(jnp.int32, (ROWS, 128), 1)
+    basis = jnp.zeros((ROWS, 128), F32)
     for j in range(RANK):
-        vector = rows[j : j + 1]
-        inner = jnp.sum(rows * vector, axis=1, keepdims=True)
-        square = inner[j : j + 1]
-        unit = vector * lax.rsqrt(square)
-        later = jnp.where(index > j, inner / square, 0.0)
-        rows = jnp.where(index == j, unit, rows - later * vector)
-    return rows
+        unit = left[j] * lax.rsqrt(jnp.sum(left[j] * left[j], axis=0, keepdims=True))
+        basis = jnp.where(lane == j, unit, basis)
+        for k in range(j + 1, RANK):
+            left[k] = left[k] - jnp.sum(unit * left[k], axis=0, keepdims=True) * unit
+    return basis
 
 
 def right_columns(split, first, second, words):
@@ -161,16 +185,17 @@
     for s in range(1, tiles_ref.shape[0]):
         total = total + tiles_ref[s]
     rows = [total[c * 2 : c * 2 + 2, q * 32 : q * 32 + 32] for c in range(2) for q in range(4)]
-    basis = orthonormal(jnp.concatenate(rows, axis=0))
-    turned_ref[...] = basis.T
-    split = jnp.concatenate(parts(basis, 3), axis=0)
+    basis = orthonormal(jnp.concatenate(rows, axis=0).T)
+    turned_ref[...] = basis[:, 0:RANK]
+    split = jnp.concatenate(parts(basis.T[0:RANK], 3), axis=0)
     split = jnp.concatenate([split, split], axis=1)
     base = lax.axis_index("c") * HALF
     for i in range(HALF // STEP):
         at = pl.ds(pl.multiple_of(base + i * STEP, STEP), STEP)
         sent = right_columns(split, grad_ref[:, at], res_ref[:, at], words_ref[:, at])
-        high, low = parts(other_ref[0:ROWS, at], 2)
-        sent = sent + right_columns(split, high, low, other_ref[ROWS : ROWS + 8, at].astype(jnp.int32))
+        high, low = parts(merged_of(other_ref, pl.multiple_of(base + i * STEP, STEP), STEP), 2)
+        words = other_ref[:, 4 * FF + i * STEP : 4 * FF + i * STEP + STEP].astype(jnp.int32)
+        sent = sent + right_columns(split, high, low, words)
         for t in range(STEP // BLOCK):
             o_ref[i * (STEP // BLOCK) + t] = sent[:, t * BLOCK : t * BLOCK + BLOCK]
 
@@ -200,16 +225,19 @@
 
 
 def update_second(
-    turned_ref, grad_ref, res_ref, own_ref, rest_ref, done_ref, q_ref, o_ref, made_ref, sems
+    turned_ref, grad_ref, res_ref, own_ref, rest_ref, done_ref, far_q_ref, o_ref, made_ref, sems, q_ref, q_sem
 ):
     c = lax.axis_index("c")
     device = ((lax.axis_index("zh") * 2 + lax.axis_index("zl")) * 16 + lax.axis_index("s")) * 2 + c
     block, offset = device // 16, (device % 16) * 40
-    copies = new_columns(1 - c, turned_ref, grad_ref, res_ref, rest_ref, o_ref, made_ref, sems)
     t = block % 16
     mine = jnp.where(block // 16 == c, own_ref[t], rest_ref[t])
     mine = pltpu.roll(mine, (BLOCK - offset) % BLOCK, 1)
     q_ref[...] = mine[:, 0:40] * WORLD ** (-0.5)
+    copy_q = pltpu.make_async_copy(q_ref, far_q_ref, q_sem)
+    copy_q.start()
+    copies = new_columns(1 - c, turned_ref, grad_ref, res_ref, rest_ref, o_ref, made_ref, sems)
+    copy_q.wait()
     for copy in copies:
         copy.wait()
 
@@ -229,16 +257,17 @@
     with jax.named_scope("share"):
         mine = call(
             share,
-            jax.ShapeDtypeStruct((ROWS + 8, FF + 128), F32),
+            jax.ShapeDtypeStruct((8, 4 * FF + HALF + 128), F32),
             limit=56 * 1024 * 1024,
-            in_specs=[far, far, far, whole],
+            in_specs=[far] * 4,
             out_specs=far,
             scratch_shapes=[
                 pltpu.VMEM((ROWS, FF), BF16),
                 pltpu.VMEM((ROWS, FF), BF16),
-                pltpu.VMEM((8, FF), jnp.int32),
-                pltpu.VMEM((ROWS + 8, FF + 128), F32),
-                pltpu.SemaphoreType.DMA((FF // SHARE, 4)),
+                pltpu.VMEM((8, HALF), jnp.int32),
+                pltpu.VMEM((RANK, ROWS), jnp.int32),
+                pltpu.VMEM((8, 4 * FF + HALF + 128), F32),
+                pltpu.SemaphoreType.DMA((FF // SHARE, 7)),
             ],
         )(grad, res, q_words, p_words)
         other = lax.ppermute(mine, "c", swap)
@@ -285,8 +314,8 @@
             update_second,
             (jax.ShapeDtypeStruct((16, 40), F32), done),
             in_specs=[whole] * 5 + [far],
-            out_specs=(whole, far),
-            scratch_shapes=room,
+            out_specs=(far, far),
+            scratch_shapes=room + [pltpu.VMEM((16, 40), F32), pltpu.SemaphoreType.DMA],
             input_output_aliases={5: 1},
         )(turned, grad, res, total, rest, updated)
     return (q_next.T, updated[None])

time: 139 us -> 136 us (0.978)
  Pallas kernels: 12 us -> 9.82 us
  transfers between devices with their start and end apart: 3 -> 3, of which waited for: 2 -> 2; matrix products, arithmetic and copies ran while one was open for 0% -> 0% of each run, Pallas kernels for 4% -> 3%
where the time goes in v6:
time: 136 us
  blocking collectives  92.2 us (68%)
  starting transfers between devices  26.1 us (19%)
  Pallas kernels  9.82 us (7%)
  waiting for transfers between devices  6.23 us (5%)
    all_to_all x6, blocking collectives, exchange(): return lax.all_to_all(blocks, axis, 0, 0, tiled=True)  92.2 us
    all_to_all x1, starting transfers between devices, exchange(): return lax.all_to_all(blocks, axis, 0, 0, tiled=True)  15.7 us
    ppermute x1, starting transfers between devices, shards(): rest = lax.ppermute(total, 'c', swap)  7.5 us
    all_to_all x1, waiting for transfers between devices, exchange(): return lax.all_to_all(blocks, axis, 0, 0, tiled=True)  5.69 us
    pallas_call x1, Pallas kernels, shards(): call(share, jax.ShapeDtypeStruct((8, 4 * FF + HALF + 128), F32), limit=56...  2.95 us
    ppermute x1, starting transfers between devices, shards(): other = lax.ppermute(mine, 'c', swap)  2.86 us
  transfers between devices with their start and end apart: 3, of which 2 were waited for; matrix products, arithmetic and copies ran while one was open for 0% of the time, Pallas kernels for 3%

profile of v6, /device:TPU:1, one launch (start us, length us, event | category | flops | bytes accessed | tf_op | source)
XLA Modules:
  0.0 135.8 jit_solution(3482509383676811344)
XLA Ops:
  0.6 0.0 copy-start.4
  0.6 0.7 copy-done.4
  1.3 0.7 gather_q_prev.2
  2.0 15.7 %all-to-all-start = ((f32[16,1,640]{2,1,0:T(1,128)}), f32[16,1,640]{2,1,0:T(1,128)S(1)}, u32[]{:S(2)}, u32[]{:S(2)}) async-start(f32[16,1,640]{2,1,0:T(1,128)} %gather_q_prev.2), calls=%async_computation | async-start | bytes 81920 | tf_op jit(solution)/shard_map/gather_q_prev/all_to_all | solution.py:246
  17.8 3.0 %share.1 = f32[8,92288]{1,0:T(8,128)} custom-call(bf16[32,20480]{1,0:T(8,128)(2,1)} %bitcast.13, bf16[32,20480]{1,0:T(8,128)(2,1)} %bitcast.18, s32[8,20480]{1,0:T(8,128)} %bitcast.26, s32[16,32]{1,0:T(8,128)} %bitcast.29), custom_call_target="tpu_custom_call" | custom-call | tf_op jit(solution)/shard_map/share/pallas_call | solution.py:258
  20.7 2.9 %collective-permute-start = (f32[8,92288]{1,0:T(8,128)}, f32[8,92288]{1,0:T(8,128)S(1)}, u32[]{:S(2)}, u32[]{:S(2)}) collective-permute-start(f32[8,92288]{1,0:T(8,128)} %share.1), channel_id=1, source_target_pairs={{0,1},{1,0},{2,3},{3,2},{4,5},{5,4},{6,7},{7,6},{8,9},{9,8},{10,11... | collective-permute-start | bytes 8859656 | tf_op jit(solution)/shard_map/share/ppermute | solution.py:273
  23.6 5.7 %all-to-all-done.x_ref = f32[16,1,640]{2,1,0:T(1,128)S(1)} async-done(((f32[16,1,640]{2,1,0:T(1,128)}), f32[16,1,640]{2,1,0:T(1,128)S(1)}, u32[]{:S(2)}, u32[]{:S(2)}) %all-to-all-start) | async-done | bytes 40992 | tf_op jit(solution)/shard_map/gather_q_prev/all_to_all | solution.py:246
  29.3 0.2 gather_q_prev.3
  29.5 0.0 copy-start
  29.5 22.0 %all_to_all.35.factor_ref = f32[32,40,128]{2,1,0:T(8,128)S(1)} all-to-all(f32[32,40,128]{2,1,0:T(8,128)S(1)} %gather_q_prev.3), channel_id=1, replica_groups=mesh['zh'=8,'zl'=2,'s'=16,'c'=2] {'s','c'}, dimensions={0} | all-to-all | bytes 1310720 | tf_op jit(solution)/shard_map/gather_q_prev/all_to_all | solution.py:246
  51.5 0.0 collective-permute-done.other_ref
  51.5 1.8 %left_factor.2 = f32[32,2,128]{2,1,0:T(2,128)S(1)} custom-call(bf16[32,20480]{1,0:T(8,128)(2,1)S(1)} %bitcast.14, bf16[32,20480]{1,0:T(8,128)(2,1)S(1)} %bitcast.19, f32[8,92288]{1,0:T(8,128)S(1)} %collective-permute-done.other_ref, f32[32,40,128]{2,1,0:T(8,128)S(1)} %all_to_all.35.factor_ref, s32[16,32]{1,0:T(8,128)S(1)} %bitcast.30), custom_call_target="tpu_custom_call" | custom-call | tf_op jit(solution)/shard_map/left_factor/pallas_call | solution.py:286
  53.3 10.8 %all_to_all.36.x_ref = f32[32,2,128]{2,1,0:T(2,128)S(1)} all-to-all(f32[32,2,128]{2,1,0:T(2,128)S(1)} %left_factor.2), channel_id=1, replica_groups=mesh['zh'=8,'zl'=2,'s'=16,'c'=2] {'s','c'}, dimensions={0} | all-to-all | bytes 65536 | tf_op jit(solution)/shard_map/left_factor/all_to_all | solution.py:246
  64.2 15.4 %all_to_all.37.tiles_ref = f32[16,4,128]{2,1,0:T(4,128)S(1)} all-to-all(f32[16,4,128]{2,1,0:T(4,128)S(1)} %left_factor.3), channel_id=1, replica_groups=mesh['zh'=8,'zl'=2,'s'=16,'c'=2] {'zh','zl'}, dimensions={0} | all-to-all | bytes 65536 | tf_op jit(solution)/shard_map/left_factor/all_to_all | solution.py:246
  79.6 1.7 %right_factor.3 = (f32[32,16]{1,0:T(8,128)S(1)}, f32[16,16,640]{2,1,0:T(8,128)S(1)}) custom-call(f32[16,4,128]{2,1,0:T(4,128)S(1)} %all_to_all.37.tiles_ref, bf16[32,20480]{1,0:T(8,128)(2,1)S(1)} %bitcast.15, bf16[32,20480]{1,0:T(8,128)(2,1)S(1)} %bitcast.20, s32[8,20480]{1,0:T(8,128)S(1)} %bitcast.27, f32[8,92288]{1,0:T(8,128)S(1)} %collective-permute-done.other_ref), custom_call_target="tpu_custom_call" | custom-call | tf_op jit(solution)/shard_map/right_factor/pallas_call | solution.py:294
  81.3 13.5 %all_to_all.38.x_ref = f32[32,8,640]{2,1,0:T(8,128)S(1)} all-to-all(f32[32,8,640]{2,1,0:T(8,128)S(1)} %bitcast.28), channel_id=1, replica_groups=mesh['zh'=8,'zl'=2,'s'=16,'c'=2] {'zl','s'}, dimensions={0} | all-to-all | bytes 1310720 | tf_op jit(solution)/shard_map/right_factor/all_to_all | solution.py:246
  94.8 0.1 right_factor.4
  94.9 17.2 %all_to_all.39.x_ref = f32[8,8,640]{2,1,0:T(8,128)S(1)} all-to-all(f32[8,8,640]{2,1,0:T(8,128)S(1)} %right_factor.4), channel_id=1, replica_groups=mesh['zh'=8,'zl'=2,'s'=16,'c'=2] {'zh'}, dimensions={0} | all-to-all | bytes 327680 | tf_op jit(solution)/shard_map/right_factor/all_to_all | solution.py:246
  112.1 0.1 right_factor.5
  112.1 13.3 %all_to_all.40 = f32[32,8,640]{2,1,0:T(8,128)S(1)} all-to-all(f32[32,8,640]{2,1,0:T(8,128)S(1)} %right_factor.5), channel_id=1, replica_groups=mesh['zh'=8,'zl'=2,'s'=16,'c'=2] {'zl','s'}, dimensions={0} | all-to-all | bytes 1310720 | tf_op jit(solution)/shard_map/right_factor/all_to_all | solution.py:246
  125.4 7.5 %collective-permute-start.1 = (f32[16,16,640]{2,1,0:T(8,128)S(1)}, f32[16,16,640]{2,1,0:T(8,128)S(1)}, u32[]{:S(2)}, u32[]{:S(2)}) collective-permute-start(f32[16,16,640]{2,1,0:T(8,128)S(1)} %bitcast.23), channel_id=1, source_target_pairs={{0,1},{1,0},{2,3},{3,2},{4,5},{5,4},{6,7},{7,6},{8,9},{9,8},{10,11... | collective-permute-start | bytes 1966088 | tf_op jit(solution)/shard_map/right_factor/ppermute | solution.py:306
  132.9 1.2 update.2.done_ref
  134.1 0.5 collective-permute-done.1.rest_ref
  134.6 1.2 update.3
  (8 shorter events, 0.0 us)
Async XLA Ops:
  0.6 0.7 copy-start.4
  2.0 27.3 %all-to-all-start = ((f32[16,1,640]{2,1,0:T(1,128)}), f32[16,1,640]{2,1,0:T(1,128)S(1)}, u32[]{:S(2)}, u32[]{:S(2)}) async-start(f32[16,1,640]{2,1,0:T(1,128)} %gather_q_prev.2), calls=%async_computation | async-start | bytes 81920 | tf_op jit(solution)/shard_map/gather_q_prev/all_to_all | solution.py:246
  20.7 30.7 %collective-permute-start = (f32[8,92288]{1,0:T(8,128)}, f32[8,92288]{1,0:T(8,128)S(1)}, u32[]{:S(2)}, u32[]{:S(2)}) collective-permute-start(f32[8,92288]{1,0:T(8,128)} %share.1), channel_id=1, source_target_pairs={{0,1},{1,0},{2,3},{3,2},{4,5},{5,4},{6,7},{7,6},{8,9},{9,8},{10,11... | collective-permute-start | bytes 8859656 | tf_op jit(solution)/shard_map/share/ppermute | solution.py:273
  29.3 22.2 %copy-start.1 = (bf16[1,32,20480]{2,1,0:T(8,128)(2,1)S(1)}, bf16[1,32,20480]{2,1,0:T(8,128)(2,1)}, u32[]{:S(2)}) copy-start(bf16[1,32,20480]{2,1,0:T(8,128)(2,1)} %param.6) | copy-start | bytes 3932164
  29.3 22.2 %copy-start.3 = (s32[1,32,16]{1,2,0:T(8,128)S(1)}, s32[1,32,16]{1,2,0:T(8,128)}, u32[]{:S(2)}) copy-start(s32[1,32,16]{1,2,0:T(8,128)} %param.8) | copy-start | bytes 6148
  29.5 22.0 %copy-start = (bf16[1,32,20480]{2,1,0:T(8,128)(2,1)S(1)}, bf16[1,32,20480]{2,1,0:T(8,128)(2,1)}, u32[]{:S(2)}) copy-start(bf16[1,32,20480]{2,1,0:T(8,128)(2,1)} %param.5) | copy-start | bytes 3932164
  51.5 28.1 %copy-start.2 = (s32[1,20480,8]{1,2,0:T(8,128)S(1)}, s32[1,20480,8]{1,2,0:T(8,128)}, u32[]{:S(2)}) copy-start(s32[1,20480,8]{1,2,0:T(8,128)} %param.9) | copy-start | bytes 1966084
  125.4 9.2 %collective-permute-start.1 = (f32[16,16,640]{2,1,0:T(8,128)S(1)}, f32[16,16,640]{2,1,0:T(8,128)S(1)}, u32[]{:S(2)}, u32[]{:S(2)}) collective-permute-start(f32[16,16,640]{2,1,0:T(8,128)S(1)} %bitcast.23), channel_id=1, source_target_pairs={{0,1},{1,0},{2,3},{3,2},{4,5},{5,4},{6,7},{7,6},{8,9},{9,8},{10,11... | collective-permute-start | bytes 1966088 | tf_op jit(solution)/shard_map/right_factor/ppermute | solution.py:306

commit v7 on v6

--- a/solution.py
+++ b/solution.py
@@ -14,8 +14,9 @@
 HALF = FF // 2
 BLOCK = 640
 STEP = 2560
-SHARE = 5120
+SHARES = ((0, 5120), (5120, 6144), (11264, 6144), (17408, 3072))
 WIDTH = 0.25
+SHORT = [[0, 2, 4, 6, 9, 11, 13, 15], [1, 3, 5, 7, 8, 10, 12, 14]]
 F32 = jnp.float32
 BF16 = jnp.bfloat16
 VMEM_LIMIT = 16 * 1024 * 1024
@@ -50,9 +51,12 @@
 ):
     theirs = pl.multiple_of((1 - lax.axis_index("c")) * HALF, HALF)
     words = pltpu.make_async_copy(far_words_ref.at[:, pl.ds(theirs, HALF)], words_ref, sems.at[0, 2])
+    late_bits = pltpu.make_async_copy(far_bits_ref, bits_ref, sems.at[2, 2])
+    words.start()
+    late_bits.start()
     copies = []
-    for i in range(FF // SHARE):
-        at = pl.ds(i * SHARE, SHARE)
+    for i, (start, size) in enumerate(SHARES):
+        at = pl.ds(start, size)
         copies.append(
             [
                 pltpu.make_async_copy(far_grad_ref.at[:, at], grad_ref.at[:, at], sems.at[i, 0]),
@@ -61,9 +65,6 @@
         )
         for copy in copies[i]:
             copy.start()
-    words.start()
-    late_bits = pltpu.make_async_copy(far_bits_ref, bits_ref, sems.at[2, 2])
-    late_bits.start()
     sent = []
 
     def send(start, size, sem):
@@ -71,20 +72,20 @@
         sent.append(pltpu.make_async_copy(o_ref.at[:, at], far_ref.at[:, at], sem))
         sent[-1].start()
 
-    for i in range(FF // SHARE):
-        at = pl.ds(i * SHARE, SHARE)
+    words.wait()
+    late_bits.wait()
+    o_ref[:, 4 * FF : 4 * FF + HALF] = words_ref[...].astype(F32)
+    bits = bits_ref[...].astype(F32)
+    o_ref[:, 4 * FF + HALF :] = jnp.concatenate([bits[0:8], bits[8:16], jnp.zeros((8, 64), F32)], axis=1)
+    send(4 * FF, HALF + 128, sems.at[1, 2])
+    for i, (start, size) in enumerate(SHARES):
+        at = pl.ds(start, size)
         for copy in copies[i]:
             copy.wait()
         merged = grad_ref[:, at].astype(F32) + res_ref[:, at].astype(F32)
         for k in range(4):
-            o_ref[:, k * FF + i * SHARE : k * FF + i * SHARE + SHARE] = merged[k * 8 : k * 8 + 8]
-            send(k * FF + i * SHARE, SHARE, sems.at[i, 3 + k])
-    words.wait()
-    late_bits.wait()
-    bits = bits_ref[...].astype(F32)
-    o_ref[:, 4 * FF + HALF :] = jnp.concatenate([bits[0:8], bits[8:16], jnp.zeros((8, 64), F32)], axis=1)
-    o_ref[:, 4 * FF : 4 * FF + HALF] = words_ref[...].astype(F32)
-    send(4 * FF, HALF + 128, sems.at[1, 2])
+            o_ref[:, k * FF + start : k * FF + start + size] = merged[k * 8 : k * 8 + 8]
+            send(k * FF + start, size, sems.at[i, 3 + k])
     for copy in sent:
         copy.wait()
 
@@ -190,6 +191,7 @@
     split = jnp.concatenate(parts(basis.T[0:RANK], 3), axis=0)
     split = jnp.concatenate([split, split], axis=1)
     base = lax.axis_index("c") * HALF
+    turn = lax.axis_index("zh") // 4 * 8
     for i in range(HALF // STEP):
         at = pl.ds(pl.multiple_of(base + i * STEP, STEP), STEP)
         sent = right_columns(split, grad_ref[:, at], res_ref[:, at], words_ref[:, at])
@@ -197,17 +199,18 @@
         words = other_ref[:, 4 * FF + i * STEP : 4 * FF + i * STEP + STEP].astype(jnp.int32)
         sent = sent + right_columns(split, high, low, words)
         for t in range(STEP // BLOCK):
-            o_ref[i * (STEP // BLOCK) + t] = sent[:, t * BLOCK : t * BLOCK + BLOCK]
+            o_ref[(i * (STEP // BLOCK) + t + turn) % 16] = sent[:, t * BLOCK : t * BLOCK + BLOCK]
 
 
 def new_columns(side, turned_ref, grad_ref, res_ref, total_ref, o_ref, made_ref, sems):
     high, low = parts(turned_ref[...] * (1.0 / WORLD), 2)
     left = jnp.concatenate([high, low, high], axis=1)
+    turn = lax.axis_index("zh") // 4 * 8
     copies = []
     for i in range(HALF // STEP):
         at = pl.ds(pl.multiple_of(side * HALF + i * STEP, STEP), STEP)
         here = pl.ds(i * STEP, STEP)
-        blocks = [total_ref[t] for t in range(i * STEP // BLOCK, (i + 1) * STEP // BLOCK)]
+        blocks = [total_ref[(t + turn) % 16] for t in range(i * STEP // BLOCK, (i + 1) * STEP // BLOCK)]
         th, tl = parts(jnp.concatenate(blocks, axis=1), 2)
         right = jnp.concatenate([th, th, tl], axis=0)
         approx = jnp.dot(left, right, preferred_element_type=F32)
@@ -230,7 +233,7 @@
     c = lax.axis_index("c")
     device = ((lax.axis_index("zh") * 2 + lax.axis_index("zl")) * 16 + lax.axis_index("s")) * 2 + c
     block, offset = device // 16, (device % 16) * 40
-    t = block % 16
+    t = (block + lax.axis_index("zh") // 4 * 8) % 16
     mine = jnp.where(block // 16 == c, own_ref[t], rest_ref[t])
     mine = pltpu.roll(mine, (BLOCK - offset) % BLOCK, 1)
     q_ref[...] = mine[:, 0:40] * WORLD ** (-0.5)
@@ -242,8 +245,8 @@
         copy.wait()
 
 
-def exchange(blocks, axis):
-    return lax.all_to_all(blocks, axis, 0, 0, tiled=True)
+def exchange(blocks, axis, groups=None):
+    return lax.all_to_all(blocks, axis, 0, 0, tiled=True, axis_index_groups=groups)
 
 
 def shards(gradient, residual, q_prev, p_bits, q_bits):
@@ -267,7 +270,7 @@
                 pltpu.VMEM((8, HALF), jnp.int32),
                 pltpu.VMEM((RANK, ROWS), jnp.int32),
                 pltpu.VMEM((8, 4 * FF + HALF + 128), F32),
-                pltpu.SemaphoreType.DMA((FF // SHARE, 7)),
+                pltpu.SemaphoreType.DMA((len(SHARES), 7)),
             ],
         )(grad, res, q_words, p_words)
         other = lax.ppermute(mine, "c", swap)
@@ -300,7 +303,7 @@
         summed = summed.reshape(32, 8, BLOCK)
         summed = exchange(summed, group)
         summed = call(add_and_repeat, jax.ShapeDtypeStruct((8, 8, BLOCK), F32), in_specs=[whole], out_specs=whole)(summed)
-        summed = exchange(summed, "zh")
+        summed = exchange(summed, z, SHORT)
         summed = call(add_and_repeat, jax.ShapeDtypeStruct((32, 8, BLOCK), F32), in_specs=[whole], out_specs=whole)(summed)
         total = exchange(summed, group).reshape(16, 16, BLOCK)
         rest = lax.ppermute(total, "c", swap)

time: 136 us -> 136 us (level)
  no operation moved by 1% of the time
where the time goes in v7:
time: 136 us
  blocking collectives  92.4 us (68%)
  starting transfers between devices  26 us (19%)
  Pallas kernels  9.86 us (7%)
  waiting for transfers between devices  6.2 us (5%)
    all_to_all x6, blocking collectives, exchange(): lax.all_to_all(blocks, axis, 0, 0, tiled=True, axis_index_groups=groups)  92.4 us
    all_to_all x1, starting transfers between devices, exchange(): lax.all_to_all(blocks, axis, 0, 0, tiled=True, axis_index_groups=groups)  15.7 us
    ppermute x1, starting transfers between devices, shards(): rest = lax.ppermute(total, 'c', swap)  7.39 us
    all_to_all x1, waiting for transfers between devices, exchange(): lax.all_to_all(blocks, axis, 0, 0, tiled=True, axis_index_groups=groups)  5.65 us
    pallas_call x1, Pallas kernels, shards(): call(share, jax.ShapeDtypeStruct((8, 4 * FF + HALF + 128), F32), limit=56...  2.99 us
    ppermute x1, starting transfers between devices, shards(): other = lax.ppermute(mine, 'c', swap)  2.86 us
  transfers between devices with their start and end apart: 3, of which 2 were waited for; matrix products, arithmetic and copies ran while one was open for 0% of the time, Pallas kernels for 3%

profile of v7, /device:TPU:1, one launch (start us, length us, event | category | flops | bytes accessed | tf_op | source)
XLA Modules:
  0.0 135.9 jit_solution(3207382954336959183)
XLA Ops:
  0.6 0.0 copy-start.4
  0.6 0.7 copy-done.4
  1.3 0.7 gather_q_prev.2
  2.0 15.7 %all-to-all-start = ((f32[16,1,640]{2,1,0:T(1,128)}), f32[16,1,640]{2,1,0:T(1,128)S(1)}, u32[]{:S(2)}, u32[]{:S(2)}) async-start(f32[16,1,640]{2,1,0:T(1,128)} %gather_q_prev.2), calls=%async_computation | async-start | bytes 81920 | tf_op jit(solution)/shard_map/gather_q_prev/all_to_all | solution.py:249
  17.8 3.0 %share.1 = f32[8,92288]{1,0:T(8,128)} custom-call(bf16[32,20480]{1,0:T(8,128)(2,1)} %bitcast.13, bf16[32,20480]{1,0:T(8,128)(2,1)} %bitcast.18, s32[8,20480]{1,0:T(8,128)} %bitcast.26, s32[16,32]{1,0:T(8,128)} %bitcast.29), custom_call_target="tpu_custom_call" | custom-call | tf_op jit(solution)/shard_map/share/pallas_call | solution.py:261
  20.8 2.9 %collective-permute-start = (f32[8,92288]{1,0:T(8,128)}, f32[8,92288]{1,0:T(8,128)S(1)}, u32[]{:S(2)}, u32[]{:S(2)}) collective-permute-start(f32[8,92288]{1,0:T(8,128)} %share.1), channel_id=1, source_target_pairs={{0,1},{1,0},{2,3},{3,2},{4,5},{5,4},{6,7},{7,6},{8,9},{9,8},{10,11... | collective-permute-start | bytes 8859656 | tf_op jit(solution)/shard_map/share/ppermute | solution.py:276
  23.7 5.6 %all-to-all-done.x_ref = f32[16,1,640]{2,1,0:T(1,128)S(1)} async-done(((f32[16,1,640]{2,1,0:T(1,128)}), f32[16,1,640]{2,1,0:T(1,128)S(1)}, u32[]{:S(2)}, u32[]{:S(2)}) %all-to-all-start) | async-done | bytes 40992 | tf_op jit(solution)/shard_map/gather_q_prev/all_to_all | solution.py:249
  29.3 0.2 gather_q_prev.3
  29.5 0.0 copy-start
  29.5 22.0 %all_to_all.35.factor_ref = f32[32,40,128]{2,1,0:T(8,128)S(1)} all-to-all(f32[32,40,128]{2,1,0:T(8,128)S(1)} %gather_q_prev.3), channel_id=1, replica_groups=mesh['zh'=8,'zl'=2,'s'=16,'c'=2] {'s','c'}, dimensions={0} | all-to-all | bytes 1310720 | tf_op jit(solution)/shard_map/gather_q_prev/all_to_all | solution.py:249
  51.5 0.0 collective-permute-done.other_ref
  51.5 1.8 %left_factor.2 = f32[32,2,128]{2,1,0:T(2,128)S(1)} custom-call(bf16[32,20480]{1,0:T(8,128)(2,1)S(1)} %bitcast.14, bf16[32,20480]{1,0:T(8,128)(2,1)S(1)} %bitcast.19, f32[8,92288]{1,0:T(8,128)S(1)} %collective-permute-done.other_ref, f32[32,40,128]{2,1,0:T(8,128)S(1)} %all_to_all.35.factor_ref, s32[16,32]{1,0:T(8,128)S(1)} %bitcast.30), custom_call_target="tpu_custom_call" | custom-call | tf_op jit(solution)/shard_map/left_factor/pallas_call | solution.py:289
  53.3 10.8 %all_to_all.36.x_ref = f32[32,2,128]{2,1,0:T(2,128)S(1)} all-to-all(f32[32,2,128]{2,1,0:T(2,128)S(1)} %left_factor.2), channel_id=1, replica_groups=mesh['zh'=8,'zl'=2,'s'=16,'c'=2] {'s','c'}, dimensions={0} | all-to-all | bytes 65536 | tf_op jit(solution)/shard_map/left_factor/all_to_all | solution.py:249
  64.2 15.5 %all_to_all.37.tiles_ref = f32[16,4,128]{2,1,0:T(4,128)S(1)} all-to-all(f32[16,4,128]{2,1,0:T(4,128)S(1)} %left_factor.3), channel_id=1, replica_groups=mesh['zh'=8,'zl'=2,'s'=16,'c'=2] {'zh','zl'}, dimensions={0} | all-to-all | bytes 65536 | tf_op jit(solution)/shard_map/left_factor/all_to_all | solution.py:249
  79.6 1.7 %right_factor.3 = (f32[32,16]{1,0:T(8,128)S(1)}, f32[16,16,640]{2,1,0:T(8,128)S(1)}) custom-call(f32[16,4,128]{2,1,0:T(4,128)S(1)} %all_to_all.37.tiles_ref, bf16[32,20480]{1,0:T(8,128)(2,1)S(1)} %bitcast.15, bf16[32,20480]{1,0:T(8,128)(2,1)S(1)} %bitcast.20, s32[8,20480]{1,0:T(8,128)S(1)} %bitcast.27, f32[8,92288]{1,0:T(8,128)S(1)} %collective-permute-done.other_ref), custom_call_target="tpu_custom_call" | custom-call | tf_op jit(solution)/shard_map/right_factor/pallas_call | solution.py:297
  81.4 13.5 %all_to_all.38.x_ref = f32[32,8,640]{2,1,0:T(8,128)S(1)} all-to-all(f32[32,8,640]{2,1,0:T(8,128)S(1)} %bitcast.28), channel_id=1, replica_groups=mesh['zh'=8,'zl'=2,'s'=16,'c'=2] {'zl','s'}, dimensions={0} | all-to-all | bytes 1310720 | tf_op jit(solution)/shard_map/right_factor/all_to_all | solution.py:249
  94.8 0.1 right_factor.4
  94.9 14.0 %all_to_all.39.x_ref = f32[8,8,640]{2,1,0:T(8,128)S(1)} all-to-all(f32[8,8,640]{2,1,0:T(8,128)S(1)} %right_factor.4), channel_id=1, replica_groups={{0,64,128,192,288,352,416,480},{32,96,160,224,256,320,384,448},{1,65,12..., dimensions={0} | all-to-all | bytes 327680 | tf_op jit(solution)/shard_map/right_factor/all_to_all | solution.py:249
  108.9 0.1 right_factor.5
  109.0 16.6 %all_to_all.40 = f32[32,8,640]{2,1,0:T(8,128)S(1)} all-to-all(f32[32,8,640]{2,1,0:T(8,128)S(1)} %right_factor.5), channel_id=1, replica_groups=mesh['zh'=8,'zl'=2,'s'=16,'c'=2] {'zl','s'}, dimensions={0} | all-to-all | bytes 1310720 | tf_op jit(solution)/shard_map/right_factor/all_to_all | solution.py:249
  125.6 7.4 %collective-permute-start.1 = (f32[16,16,640]{2,1,0:T(8,128)S(1)}, f32[16,16,640]{2,1,0:T(8,128)S(1)}, u32[]{:S(2)}, u32[]{:S(2)}) collective-permute-start(f32[16,16,640]{2,1,0:T(8,128)S(1)} %bitcast.23), channel_id=1, source_target_pairs={{0,1},{1,0},{2,3},{3,2},{4,5},{5,4},{6,7},{7,6},{8,9},{9,8},{10,11... | collective-permute-start | bytes 1966088 | tf_op jit(solution)/shard_map/right_factor/ppermute | solution.py:309
  133.0 1.1 update.2.done_ref
  134.1 0.5 collective-permute-done.1.rest_ref
  134.7 1.2 update.3
  (8 shorter events, 0.0 us)
Async XLA Ops:
  0.6 0.7 copy-start.4
  2.0 27.3 %all-to-all-start = ((f32[16,1,640]{2,1,0:T(1,128)}), f32[16,1,640]{2,1,0:T(1,128)S(1)}, u32[]{:S(2)}, u32[]{:S(2)}) async-start(f32[16,1,640]{2,1,0:T(1,128)} %gather_q_prev.2), calls=%async_computation | async-start | bytes 81920 | tf_op jit(solution)/shard_map/gather_q_prev/all_to_all | solution.py:249
  20.8 30.7 %collective-permute-start = (f32[8,92288]{1,0:T(8,128)}, f32[8,92288]{1,0:T(8,128)S(1)}, u32[]{:S(2)}, u32[]{:S(2)}) collective-permute-start(f32[8,92288]{1,0:T(8,128)} %share.1), channel_id=1, source_target_pairs={{0,1},{1,0},{2,3},{3,2},{4,5},{5,4},{6,7},{7,6},{8,9},{9,8},{10,11... | collective-permute-start | bytes 8859656 | tf_op jit(solution)/shard_map/share/ppermute | solution.py:276
  29.3 22.2 %copy-start.1 = (bf16[1,32,20480]{2,1,0:T(8,128)(2,1)S(1)}, bf16[1,32,20480]{2,1,0:T(8,128)(2,1)}, u32[]{:S(2)}) copy-start(bf16[1,32,20480]{2,1,0:T(8,128)(2,1)} %param.6) | copy-start | bytes 3932164
  29.3 22.2 %copy-start.3 = (s32[1,32,16]{1,2,0:T(8,128)S(1)}, s32[1,32,16]{1,2,0:T(8,128)}, u32[]{:S(2)}) copy-start(s32[1,32,16]{1,2,0:T(8,128)} %param.8) | copy-start | bytes 6148
  29.5 22.0 %copy-start = (bf16[1,32,20480]{2,1,0:T(8,128)(2,1)S(1)}, bf16[1,32,20480]{2,1,0:T(8,128)(2,1)}, u32[]{:S(2)}) copy-start(bf16[1,32,20480]{2,1,0:T(8,128)(2,1)} %param.5) | copy-start | bytes 3932164
  51.5 28.2 %copy-start.2 = (s32[1,20480,8]{1,2,0:T(8,128)S(1)}, s32[1,20480,8]{1,2,0:T(8,128)}, u32[]{:S(2)}) copy-start(s32[1,20480,8]{1,2,0:T(8,128)} %param.9) | copy-start | bytes 1966084
  125.6 9.1 %collective-permute-start.1 = (f32[16,16,640]{2,1,0:T(8,128)S(1)}, f32[16,16,640]{2,1,0:T(8,128)S(1)}, u32[]{:S(2)}, u32[]{:S(2)}) collective-permute-start(f32[16,16,640]{2,1,0:T(8,128)S(1)} %bitcast.23), channel_id=1, source_target_pairs={{0,1},{1,0},{2,3},{3,2},{4,5},{5,4},{6,7},{7,6},{8,9},{9,8},{10,11... | collective-permute-start | bytes 1966088 | tf_op jit(solution)/shard_map/right_factor/ppermute | solution.py:309

commit v8 on v6

--- a/solution.py
+++ b/solution.py
@@ -99,24 +99,25 @@
         rows = [pieces[:, r * 40 : r * 40 + 40] for r in range(half * 8, half * 8 + 8)]
         packed = jnp.concatenate(rows, axis=0).T
         for s in range(16):
-            o_ref[s * 2 + half] = packed
+            o_ref[half * 16 + s] = packed
 
 
 def left_factor(grad_ref, res_ref, other_ref, factor_ref, bits_ref, o_ref):
     c = lax.axis_index("c")
-    factor = jnp.concatenate(parts(factor_ref[...].reshape(1280, 128), 2), axis=1)
+    whole = jnp.concatenate([factor_ref[k * 16 + s] for s in range(16) for k in range(2)], axis=0)
+    factor = jnp.concatenate(parts(whole, 2), axis=1)
     owner = lax.broadcasted_iota(jnp.int32, (ROWS, 128), 1) % 16
     totals = [jnp.zeros((ROWS, 128), F32), jnp.zeros((ROWS, 128), F32)]
-    for z in range(0, 16, 4):
-        places = [slice(k * 1280, k * 1280 + 1280) for k in range(z, z + 4)]
-        split = [parts(merged_of(other_ref, k * 1280, 1280), 2) for k in range(z, z + 4)]
+    for z in range(0, 16, 2):
+        places = [slice(k * 1280, k * 1280 + 1280) for k in range(z, z + 2)]
+        split = [parts(merged_of(other_ref, k * 1280, 1280), 2) for k in range(z, z + 2)]
         rows = [grad_ref[:, at] for at in places] + [res_ref[:, at] for at in places]
         rows += [high for high, _ in split] + [low for _, low in split]
         prod = jnp.dot(jnp.concatenate(rows, axis=0), factor, preferred_element_type=F32)
         prod = prod[:, 0:128] + prod[:, 128:256]
         for w in range(2):
-            both = prod[w * 256 : w * 256 + 128] + prod[w * 256 + 128 : w * 256 + 256]
-            for k in range(4):
+            both = prod[w * 128 : w * 128 + 64] + prod[w * 128 + 64 : w * 128 + 128]
+            for k in range(2):
                 totals[w] = totals[w] + jnp.where(owner == z + k, both[k * 32 : k * 32 + 32], 0.0)
     rank = lax.broadcasted_iota(jnp.int32, (8, 128), 0)
     lane = lax.broadcasted_iota(jnp.int32, (8, 128), 1)
@@ -142,9 +143,9 @@
 def add_left(x_ref, o_ref):
     halves = []
     for c in range(2):
-        total = x_ref[c]
+        total = x_ref[c * 16]
         for s in range(1, 16):
-            total = total + x_ref[s * 2 + c]
+            total = total + x_ref[c * 16 + s]
         halves.append(total)
     both = jnp.concatenate(halves, axis=0)
     for z in range(o_ref.shape[0]):
@@ -247,7 +248,7 @@
 
 
 def shards(gradient, residual, q_prev, p_bits, q_bits):
-    z, plane, group = ("zh", "zl"), ("s", "c"), ("zl", "s")
+    z, plane, group = ("zh", "zl"), ("c", "s"), ("zl", "s")
     grad, res = gradient[0], residual[0]
     p_words, q_words = p_bits[0].T, q_bits[0].T
     swap = [(0, 1), (1, 0)]

time: 136 us -> 136 us (level)
  no operation moved by 1% of the time
where the time goes in v8:
time: 136 us
  blocking collectives  92.2 us (68%)
  starting transfers between devices  26.1 us (19%)
  Pallas kernels  9.83 us (7%)
  waiting for transfers between devices  6.23 us (5%)
    all_to_all x6, blocking collectives, exchange(): return lax.all_to_all(blocks, axis, 0, 0, tiled=True)  92.2 us
    all_to_all x1, starting transfers between devices, exchange(): return lax.all_to_all(blocks, axis, 0, 0, tiled=True)  15.7 us
    ppermute x1, starting transfers between devices, shards(): rest = lax.ppermute(total, 'c', swap)  7.49 us
    all_to_all x1, waiting for transfers between devices, exchange(): return lax.all_to_all(blocks, axis, 0, 0, tiled=True)  5.69 us
    pallas_call x1, Pallas kernels, shards(): call(share, jax.ShapeDtypeStruct((8, 4 * FF + HALF + 128), F32), limit=56...  2.95 us
    ppermute x1, starting transfers between devices, shards(): other = lax.ppermute(mine, 'c', swap)  2.86 us
  transfers between devices with their start and end apart: 3, of which 2 were waited for; matrix products, arithmetic and copies ran while one was open for 0% of the time, Pallas kernels for 3%

profile of v8, /device:TPU:1, one launch (start us, length us, event | category | flops | bytes accessed | tf_op | source)
XLA Modules:
  0.0 135.8 jit_solution(3675130364786759658)
XLA Ops:
  0.6 0.0 copy-start.4
  0.6 0.7 copy-done.4
  1.3 0.7 gather_q_prev.2
  2.0 15.7 %all-to-all-start = ((f32[16,1,640]{2,1,0:T(1,128)}), f32[16,1,640]{2,1,0:T(1,128)S(1)}, u32[]{:S(2)}, u32[]{:S(2)}) async-start(f32[16,1,640]{2,1,0:T(1,128)} %gather_q_prev.2), calls=%async_computation | async-start | bytes 81920 | tf_op jit(solution)/shard_map/gather_q_prev/all_to_all | solution.py:247
  17.8 3.0 %share.1 = f32[8,92288]{1,0:T(8,128)} custom-call(bf16[32,20480]{1,0:T(8,128)(2,1)} %bitcast.13, bf16[32,20480]{1,0:T(8,128)(2,1)} %bitcast.18, s32[8,20480]{1,0:T(8,128)} %bitcast.26, s32[16,32]{1,0:T(8,128)} %bitcast.29), custom_call_target="tpu_custom_call" | custom-call | tf_op jit(solution)/shard_map/share/pallas_call | solution.py:259
  20.7 2.9 %collective-permute-start = (f32[8,92288]{1,0:T(8,128)}, f32[8,92288]{1,0:T(8,128)S(1)}, u32[]{:S(2)}, u32[]{:S(2)}) collective-permute-start(f32[8,92288]{1,0:T(8,128)} %share.1), channel_id=1, source_target_pairs={{0,1},{1,0},{2,3},{3,2},{4,5},{5,4},{6,7},{7,6},{8,9},{9,8},{10,11... | collective-permute-start | bytes 8859656 | tf_op jit(solution)/shard_map/share/ppermute | solution.py:274
  23.6 5.7 %all-to-all-done.x_ref = f32[16,1,640]{2,1,0:T(1,128)S(1)} async-done(((f32[16,1,640]{2,1,0:T(1,128)}), f32[16,1,640]{2,1,0:T(1,128)S(1)}, u32[]{:S(2)}, u32[]{:S(2)}) %all-to-all-start) | async-done | bytes 40992 | tf_op jit(solution)/shard_map/gather_q_prev/all_to_all | solution.py:247
  29.3 0.2 gather_q_prev.3
  29.5 0.0 copy-start
  29.5 21.3 %all_to_all.35.factor_ref = f32[32,40,128]{2,1,0:T(8,128)S(1)} all-to-all(f32[32,40,128]{2,1,0:T(8,128)S(1)} %gather_q_prev.3), channel_id=1, replica_groups=mesh['zh'=8,'zl'=2,'s'=16,'c'=2] {'c','s'}, dimensions={0} | all-to-all | bytes 1310720 | tf_op jit(solution)/shard_map/gather_q_prev/all_to_all | solution.py:247
  50.9 0.0 collective-permute-done.other_ref
  50.9 1.8 %left_factor.2 = f32[32,2,128]{2,1,0:T(2,128)S(1)} custom-call(bf16[32,20480]{1,0:T(8,128)(2,1)S(1)} %bitcast.14, bf16[32,20480]{1,0:T(8,128)(2,1)S(1)} %bitcast.19, f32[8,92288]{1,0:T(8,128)S(1)} %collective-permute-done.other_ref, f32[32,40,128]{2,1,0:T(8,128)S(1)} %all_to_all.35.factor_ref, s32[16,32]{1,0:T(8,128)S(1)} %bitcast.30), custom_call_target="tpu_custom_call" | custom-call | tf_op jit(solution)/shard_map/left_factor/pallas_call | solution.py:287
  52.7 11.2 %all_to_all.36.x_ref = f32[32,2,128]{2,1,0:T(2,128)S(1)} all-to-all(f32[32,2,128]{2,1,0:T(2,128)S(1)} %left_factor.2), channel_id=1, replica_groups=mesh['zh'=8,'zl'=2,'s'=16,'c'=2] {'c','s'}, dimensions={0} | all-to-all | bytes 65536 | tf_op jit(solution)/shard_map/left_factor/all_to_all | solution.py:247
  63.9 15.4 %all_to_all.37.tiles_ref = f32[16,4,128]{2,1,0:T(4,128)S(1)} all-to-all(f32[16,4,128]{2,1,0:T(4,128)S(1)} %left_factor.3), channel_id=1, replica_groups=mesh['zh'=8,'zl'=2,'s'=16,'c'=2] {'zh','zl'}, dimensions={0} | all-to-all | bytes 65536 | tf_op jit(solution)/shard_map/left_factor/all_to_all | solution.py:247
  79.4 1.7 %right_factor.3 = (f32[32,16]{1,0:T(8,128)S(1)}, f32[16,16,640]{2,1,0:T(8,128)S(1)}) custom-call(f32[16,4,128]{2,1,0:T(4,128)S(1)} %all_to_all.37.tiles_ref, bf16[32,20480]{1,0:T(8,128)(2,1)S(1)} %bitcast.15, bf16[32,20480]{1,0:T(8,128)(2,1)S(1)} %bitcast.20, s32[8,20480]{1,0:T(8,128)S(1)} %bitcast.27, f32[8,92288]{1,0:T(8,128)S(1)} %collective-permute-done.other_ref), custom_call_target="tpu_custom_call" | custom-call | tf_op jit(solution)/shard_map/right_factor/pallas_call | solution.py:295
  81.1 13.8 %all_to_all.38.x_ref = f32[32,8,640]{2,1,0:T(8,128)S(1)} all-to-all(f32[32,8,640]{2,1,0:T(8,128)S(1)} %bitcast.28), channel_id=1, replica_groups=mesh['zh'=8,'zl'=2,'s'=16,'c'=2] {'zl','s'}, dimensions={0} | all-to-all | bytes 1310720 | tf_op jit(solution)/shard_map/right_factor/all_to_all | solution.py:247
  94.8 0.1 right_factor.4
  94.9 17.2 %all_to_all.39.x_ref = f32[8,8,640]{2,1,0:T(8,128)S(1)} all-to-all(f32[8,8,640]{2,1,0:T(8,128)S(1)} %right_factor.4), channel_id=1, replica_groups=mesh['zh'=8,'zl'=2,'s'=16,'c'=2] {'zh'}, dimensions={0} | all-to-all | bytes 327680 | tf_op jit(solution)/shard_map/right_factor/all_to_all | solution.py:247
  112.1 0.1 right_factor.5
  112.1 13.3 %all_to_all.40 = f32[32,8,640]{2,1,0:T(8,128)S(1)} all-to-all(f32[32,8,640]{2,1,0:T(8,128)S(1)} %right_factor.5), channel_id=1, replica_groups=mesh['zh'=8,'zl'=2,'s'=16,'c'=2] {'zl','s'}, dimensions={0} | all-to-all | bytes 1310720 | tf_op jit(solution)/shard_map/right_factor/all_to_all | solution.py:247
  125.4 7.5 %collective-permute-start.1 = (f32[16,16,640]{2,1,0:T(8,128)S(1)}, f32[16,16,640]{2,1,0:T(8,128)S(1)}, u32[]{:S(2)}, u32[]{:S(2)}) collective-permute-start(f32[16,16,640]{2,1,0:T(8,128)S(1)} %bitcast.23), channel_id=1, source_target_pairs={{0,1},{1,0},{2,3},{3,2},{4,5},{5,4},{6,7},{7,6},{8,9},{9,8},{10,11... | collective-permute-start | bytes 1966088 | tf_op jit(solution)/shard_map/right_factor/ppermute | solution.py:307
  132.9 1.2 update.2.done_ref
  134.1 0.5 collective-permute-done.1.rest_ref
  134.6 1.2 update.3
  (8 shorter events, 0.0 us)
Async XLA Ops:
  0.6 0.7 copy-start.4
  2.0 27.3 %all-to-all-start = ((f32[16,1,640]{2,1,0:T(1,128)}), f32[16,1,640]{2,1,0:T(1,128)S(1)}, u32[]{:S(2)}, u32[]{:S(2)}) async-start(f32[16,1,640]{2,1,0:T(1,128)} %gather_q_prev.2), calls=%async_computation | async-start | bytes 81920 | tf_op jit(solution)/shard_map/gather_q_prev/all_to_all | solution.py:247
  20.7 30.1 %collective-permute-start = (f32[8,92288]{1,0:T(8,128)}, f32[8,92288]{1,0:T(8,128)S(1)}, u32[]{:S(2)}, u32[]{:S(2)}) collective-permute-start(f32[8,92288]{1,0:T(8,128)} %share.1), channel_id=1, source_target_pairs={{0,1},{1,0},{2,3},{3,2},{4,5},{5,4},{6,7},{7,6},{8,9},{9,8},{10,11... | collective-permute-start | bytes 8859656 | tf_op jit(solution)/shard_map/share/ppermute | solution.py:274
  29.3 21.6 %copy-start.1 = (bf16[1,32,20480]{2,1,0:T(8,128)(2,1)S(1)}, bf16[1,32,20480]{2,1,0:T(8,128)(2,1)}, u32[]{:S(2)}) copy-start(bf16[1,32,20480]{2,1,0:T(8,128)(2,1)} %param.6) | copy-start | bytes 3932164
  29.3 21.6 %copy-start.3 = (s32[1,32,16]{1,2,0:T(8,128)S(1)}, s32[1,32,16]{1,2,0:T(8,128)}, u32[]{:S(2)}) copy-start(s32[1,32,16]{1,2,0:T(8,128)} %param.8) | copy-start | bytes 6148
  29.5 21.4 %copy-start = (bf16[1,32,20480]{2,1,0:T(8,128)(2,1)S(1)}, bf16[1,32,20480]{2,1,0:T(8,128)(2,1)}, u32[]{:S(2)}) copy-start(bf16[1,32,20480]{2,1,0:T(8,128)(2,1)} %param.5) | copy-start | bytes 3932164
  50.9 28.5 %copy-start.2 = (s32[1,20480,8]{1,2,0:T(8,128)S(1)}, s32[1,20480,8]{1,2,0:T(8,128)}, u32[]{:S(2)}) copy-start(s32[1,20480,8]{1,2,0:T(8,128)} %param.9) | copy-start | bytes 1966084
  125.4 9.2 %collective-permute-start.1 = (f32[16,16,640]{2,1,0:T(8,128)S(1)}, f32[16,16,640]{2,1,0:T(8,128)S(1)}, u32[]{:S(2)}, u32[]{:S(2)}) collective-permute-start(f32[16,16,640]{2,1,0:T(8,128)S(1)} %bitcast.23), channel_id=1, source_target_pairs={{0,1},{1,0},{2,3},{3,2},{4,5},{5,4},{6,7},{7,6},{8,9},{9,8},{10,11... | collective-permute-start | bytes 1966088 | tf_op jit(solution)/shard_map/right_factor/ppermute | solution.py:307
